TPU v7x, 32 devices: a whole 2x2x4 slice. The times are simulated.
32 devices in a mesh: dp: 4 (over x, core), fsdp: 8 (over z, y).
Axes of the slice: x: 2, y: 2, z: 4, core: 2. Of those that a mesh axis runs over, the one named last changes fastest.
Arguments:
- tokens: bfloat16 [2, 16384, 768], P(None, ('dp', 'fsdp')), may hold values from -6 to 6
- lengths: int32 [2, 32], P(None, ('dp', 'fsdp')), may hold values from 256 to 512, as said below
- cotangent: bfloat16 [2, 16384, 768], P(None, ('dp', 'fsdp')), may hold values from -6 to 6
- mixer_in: bfloat16 [768, 3072], P(('dp', 'fsdp')), may hold values from -0.21875 to 0.21875
- w_eta: bfloat16 [768, 12], P(('dp', 'fsdp')), may hold values from -0.21875 to 0.21875
- eta_bias: bfloat16 [12], replicated, may hold values from -1 to 1
- w_out: bfloat16 [768, 768], P(('dp', 'fsdp')), may hold values from -0.4375 to 0.4375
- inner_w: bfloat16 [768, 64], P(('dp', 'fsdp')), may hold values from -0.75 to 0.75
- inner_b: bfloat16 [768], P(('dp', 'fsdp')), may hold values from -3 to 3
- ttt_gain: bfloat16 [768], P(('dp', 'fsdp')), may hold values from 0.5 to 1.5
- ttt_shift: bfloat16 [768], P(('dp', 'fsdp')), may hold values from -2 to 2
- norm_one: bfloat16 [768], P(('dp', 'fsdp')), may hold values from 0.5 to 1.5
- post_gain: bfloat16 [768], P(('dp', 'fsdp')), may hold values from 0.5 to 1.5
- post_shift: bfloat16 [768], P(('dp', 'fsdp')), may hold values from -2 to 2
- w_gate_up: bfloat16 [768, 4096], P(('dp', 'fsdp')), may hold values from -0.21875 to 0.21875
- w_down: bfloat16 [2048, 768], P(('dp', 'fsdp')), may hold values from -0.25 to 0.25
- norm_two: bfloat16 [768], P(('dp', 'fsdp')), may hold values from 0.5 to 1.5
Outputs:
- block_out: bfloat16 [2, 16384, 768], P(None, ('dp', 'fsdp'))
- grad_tokens: bfloat16 [2, 16384, 768], P(None, ('dp', 'fsdp'))
- grad_mixer_in: float32 [768, 3072], P(('dp', 'fsdp'))
- grad_w_eta: float32 [768, 12], P(('dp', 'fsdp'))
- grad_eta_bias: float32 [12], replicated
- grad_w_out: float32 [768, 768], P(('dp', 'fsdp'))
- grad_inner_w: float32 [768, 64], P(('dp', 'fsdp'))
- grad_inner_b: float32 [768], P(('dp', 'fsdp'))
- grad_ttt_gain: float32 [768], P(('dp', 'fsdp'))
- grad_ttt_shift: float32 [768], P(('dp', 'fsdp'))
- grad_norm_one: float32 [768], P(('dp', 'fsdp'))
- grad_post_gain: float32 [768], P(('dp', 'fsdp'))
- grad_post_shift: float32 [768], P(('dp', 'fsdp'))
- grad_w_gate_up: float32 [768, 4096], P(('dp', 'fsdp'))
- grad_w_down: float32 [2048, 768], P(('dp', 'fsdp'))
- grad_norm_two: float32 [768], P(('dp', 'fsdp'))
Inputs may be any that keep to these rules, and one draw needn't show every extreme that they name: `lengths`: every entry is a multiple of 16; some entry equals 512.
All inputs are finite; a program needn't handle non-finite values.
Results may differ from a plain program's by a relative error of at most 0.0085.
The roundings to bfloat16 on the way count: a program that leaves them out, or rounds other values in their place, can miss the bound.
Values may be sent and summed in bfloat16 or wider, within the bound.
No kernel may reach another device: no remote copies, remote signals or barrier semaphores. Data moves between devices by JAX's collectives and lax.ppermute only.
A program may use at most 256 MiB of HBM per device.

v0:
```python
import jax
import jax.numpy as jnp
from jax import lax
from jax.sharding import PartitionSpec as P

MINI = 16


epsilon = 1e-06
highest = lax.Precision.HIGHEST


def rms_norm(values, gains):
    return values * lax.rsqrt(jnp.mean(values * values, axis=-1, keepdims=True) + epsilon) * gains


def layer_norm(values, gains, shifts):
    centred = values - jnp.mean(values, axis=-1, keepdims=True)
    return (
        centred * lax.rsqrt(jnp.mean(centred * centred, axis=-1, keepdims=True) + epsilon) * gains
        + shifts
    )


def inner_step(gains, shifts, running, pieces):
    weight, offset = running
    queries, key_rows, value_rows, rates = pieces
    block_size = queries.shape[-2]
    row_ids = lax.broadcasted_iota(jnp.int32, (block_size, block_size), 0)
    col_ids = lax.broadcasted_iota(jnp.int32, (block_size, block_size), 1)
    lower_mask = (row_ids >= col_ids).astype(queries.dtype)
    token_scale = 1.0 / (row_ids[:, 0] + 1).astype(queries.dtype)
    hidden = (
        jnp.einsum("ghme,ghef->ghmf", key_rows, weight, precision=highest) + offset[:, :, None, :]
    )
    centred = hidden - jnp.mean(hidden, axis=-1, keepdims=True)
    inverse = lax.rsqrt(jnp.mean(centred * centred, axis=-1, keepdims=True) + epsilon)
    normed = centred * inverse
    residual_grad = (gains * normed + shifts - (value_rows - key_rows)) * gains
    inner_grad = (
        residual_grad
        - jnp.mean(residual_grad, axis=-1, keepdims=True)
        - normed * jnp.mean(residual_grad * normed, axis=-1, keepdims=True)
    ) * inverse
    eta_matrix = token_scale[:, None] * rates[:, :, None, :] * lower_mask
    scores = jnp.einsum("ghme,ghne->ghmn", queries, key_rows, precision=highest)
    updated = (
        jnp.einsum("ghme,ghef->ghmf", queries, weight, precision=highest)
        + offset[:, :, None, :]
        - jnp.einsum(
            "ghmn,ghnf->ghmf", eta_matrix * scores + eta_matrix, inner_grad, precision=highest
        )
    )
    last_row = eta_matrix[:, :, -1, :]
    weight_next = weight - jnp.einsum(
        "ghme,ghmf->ghef", key_rows * last_row[..., None], inner_grad, precision=highest
    )
    offset_next = offset - jnp.einsum("ghm,ghmf->ghf", last_row, inner_grad, precision=highest)
    result = queries + layer_norm(updated, gains, shifts)
    return ((weight_next, offset_next), result)


def inner_layer(queries, key_rows, value_rows, rates, inner_w, inner_b, ttt_gain, ttt_shift):
    groups, length, width = queries.shape
    heads = rates.shape[-1]
    head_size = width // heads
    blocks = length // MINI

    def split_heads(values):
        return values.reshape(groups, blocks, MINI, heads, head_size).transpose(1, 0, 3, 2, 4)

    rate_blocks = rates.reshape(groups, blocks, MINI, heads).transpose(1, 0, 3, 2)
    start = (
        jnp.broadcast_to(
            inner_w.reshape(heads, head_size, head_size), (groups, heads, head_size, head_size)
        ),
        jnp.broadcast_to(inner_b.reshape(heads, head_size), (groups, heads, head_size)),
    )
    gains = ttt_gain.reshape(heads, 1, head_size)
    shifts = ttt_shift.reshape(heads, 1, head_size)
    stepper = jax.checkpoint(lambda running, pieces: inner_step(gains, shifts, running, pieces))
    final_state, outputs = lax.scan(
        stepper,
        start,
        (split_heads(queries), split_heads(key_rows), split_heads(value_rows), rate_blocks),
    )
    return outputs.transpose(1, 0, 3, 2, 4).reshape(groups, length, width)


def mixer_core(
    projected,
    eta_linear,
    live_mask,
    eta_bias,
    inner_w,
    inner_b,
    ttt_gain,
    ttt_shift,
    post_gain,
    post_shift,
):
    width = projected.shape[-1] // 4
    heads = eta_bias.shape[0]
    rates = jax.nn.sigmoid(eta_linear + eta_bias) / (width // heads) * live_mask[:, None]
    inner_out = inner_layer(
        projected[None, :, :width],
        projected[None, :, width : 2 * width],
        projected[None, :, 2 * width : 3 * width],
        rates[None],
        inner_w,
        inner_b,
        ttt_gain,
        ttt_shift,
    )[0]
    return layer_norm(inner_out, post_gain, post_shift) * jax.nn.gelu(
        projected[:, 3 * width :], approximate=True
    )


def swiglu(both):
    half_width = both.shape[-1] // 2
    return jax.nn.silu(both[:, :half_width]) * both[:, half_width:]


def trans_dot(former, latter):
    return lax.dot_general(
        former, latter, (((0,), (0,)), ((), ())), preferred_element_type=jnp.float32
    )


def back_dot(former, latter):
    return lax.dot_general(
        former, latter, (((1,), (1,)), ((), ())), preferred_element_type=jnp.float32
    )


def fetch_mixer(
    mixer_in, w_eta, w_out, inner_w, inner_b, ttt_gain, ttt_shift, norm_one, post_gain, post_shift
):
    return (
        lax.all_gather(mixer_in, ("dp", "fsdp"), axis=0, tiled=True),
        lax.all_gather(w_eta, ("dp", "fsdp"), axis=0, tiled=True),
        lax.all_gather(w_out, ("dp", "fsdp"), axis=0, tiled=True),
        lax.all_gather(inner_w, ("dp", "fsdp"), axis=0, tiled=True),
        lax.all_gather(inner_b, ("dp", "fsdp"), axis=0, tiled=True),
        lax.all_gather(ttt_gain, ("dp", "fsdp"), axis=0, tiled=True),
        lax.all_gather(ttt_shift, ("dp", "fsdp"), axis=0, tiled=True),
        lax.all_gather(norm_one, ("dp", "fsdp"), axis=0, tiled=True),
        lax.all_gather(post_gain, ("dp", "fsdp"), axis=0, tiled=True),
        lax.all_gather(post_shift, ("dp", "fsdp"), axis=0, tiled=True),
    )


def fetch_ffn(w_gate_up, w_down, norm_two):
    return (
        lax.all_gather(w_gate_up, ("dp", "fsdp"), axis=0, tiled=True),
        lax.all_gather(w_down, ("dp", "fsdp"), axis=0, tiled=True),
        lax.all_gather(norm_two, ("dp", "fsdp"), axis=0, tiled=True),
    )


def reduce_all(mixer_terms, ffn_terms, eta_term):
    mixer_part = (
        lax.psum_scatter(mixer_terms[0], ("dp", "fsdp"), scatter_dimension=0, tiled=True),
        lax.psum_scatter(mixer_terms[1], ("dp", "fsdp"), scatter_dimension=0, tiled=True),
        lax.psum_scatter(mixer_terms[2], ("dp", "fsdp"), scatter_dimension=0, tiled=True),
        lax.psum_scatter(mixer_terms[3], ("dp", "fsdp"), scatter_dimension=0, tiled=True),
        lax.psum_scatter(mixer_terms[4], ("dp", "fsdp"), scatter_dimension=0, tiled=True),
        lax.psum_scatter(mixer_terms[5], ("dp", "fsdp"), scatter_dimension=0, tiled=True),
        lax.psum_scatter(mixer_terms[6], ("dp", "fsdp"), scatter_dimension=0, tiled=True),
        lax.psum_scatter(mixer_terms[7], ("dp", "fsdp"), scatter_dimension=0, tiled=True),
        lax.psum_scatter(mixer_terms[8], ("dp", "fsdp"), scatter_dimension=0, tiled=True),
        lax.psum_scatter(mixer_terms[9], ("dp", "fsdp"), scatter_dimension=0, tiled=True),
    )
    ffn_part = (
        lax.psum_scatter(ffn_terms[0], ("dp", "fsdp"), scatter_dimension=0, tiled=True),
        lax.psum_scatter(ffn_terms[1], ("dp", "fsdp"), scatter_dimension=0, tiled=True),
        lax.psum_scatter(ffn_terms[2], ("dp", "fsdp"), scatter_dimension=0, tiled=True),
    )
    eta_part = lax.psum(eta_term, ("dp", "fsdp"))
    return tuple(mixer_part) + tuple(ffn_part) + (eta_part,)


def add_tuples(former, latter):
    return tuple((first_item + second_item for first_item, second_item in zip(former, latter)))


def body(
    tokens,
    lengths,
    cotangent,
    mixer_in,
    w_eta,
    eta_bias,
    w_out,
    inner_w,
    inner_b,
    ttt_gain,
    ttt_shift,
    norm_one,
    post_gain,
    post_shift,
    w_gate_up,
    w_down,
    norm_two,
):
    slot_count = tokens.shape[1]
    places = lax.broadcasted_iota(jnp.int32, (slot_count,), 0)
    eta_bias_f = eta_bias.astype(jnp.float32)
    outputs_list = []
    backs_list = []
    summed = None
    for micro_index in range(tokens.shape[0]):
        mixer_set = fetch_mixer(
            mixer_in,
            w_eta,
            w_out,
            inner_w,
            inner_b,
            ttt_gain,
            ttt_shift,
            norm_one,
            post_gain,
            post_shift,
        )
        ffn_set = fetch_ffn(w_gate_up, w_down, norm_two)
        (
            whole_mixer,
            whole_eta,
            whole_out,
            whole_inner_w,
            whole_inner_b,
            whole_gain,
            whole_shift,
            whole_norm_one,
            whole_post_gain,
            whole_post_shift,
        ) = mixer_set
        whole_gate_up, whole_down, whole_norm_two = ffn_set
        live_mask = (places < lengths[micro_index, 0]).astype(jnp.float32)
        row_data = tokens[micro_index].astype(jnp.float32)
        normed_f, first_norm_pull = jax.vjp(rms_norm, row_data, whole_norm_one.astype(jnp.float32))
        normed = normed_f.astype(jnp.bfloat16)
        projected = jnp.dot(normed, whole_mixer, preferred_element_type=jnp.float32)
        eta_linear = jnp.dot(normed, whole_eta, preferred_element_type=jnp.float32)
        mixed_f, mixer_pull = jax.vjp(
            lambda proj_in, eta_in, bias_in, weight_in, offset_in, gain_in, shift_in, pgain_in, pshift_in: mixer_core(
                proj_in,
                eta_in,
                live_mask,
                bias_in,
                weight_in,
                offset_in,
                gain_in,
                shift_in,
                pgain_in,
                pshift_in,
            ),
            projected,
            eta_linear,
            eta_bias_f,
            whole_inner_w.astype(jnp.float32),
            whole_inner_b.astype(jnp.float32),
            whole_gain.astype(jnp.float32),
            whole_shift.astype(jnp.float32),
            whole_post_gain.astype(jnp.float32),
            whole_post_shift.astype(jnp.float32),
        )
        mixed_out = mixed_f.astype(jnp.bfloat16)
        first = row_data + jnp.dot(mixed_out, whole_out, preferred_element_type=jnp.float32)
        second_f, second_norm_pull = jax.vjp(rms_norm, first, whole_norm_two.astype(jnp.float32))
        second = second_f.astype(jnp.bfloat16)
        both = jnp.dot(second, whole_gate_up, preferred_element_type=jnp.float32)
        activated_f, swiglu_pull = jax.vjp(swiglu, both)
        activated = activated_f.astype(jnp.bfloat16)
        outputs_list.append(
            (first + jnp.dot(activated, whole_down, preferred_element_type=jnp.float32)).astype(
                jnp.bfloat16
            )
        )
        back_mixer, back_eta, back_out = (
            lax.all_gather(mixer_in, ("dp", "fsdp"), axis=0, tiled=True),
            lax.all_gather(w_eta, ("dp", "fsdp"), axis=0, tiled=True),
            lax.all_gather(w_out, ("dp", "fsdp"), axis=0, tiled=True),
        )
        back_gate_up, back_down = (
            lax.all_gather(w_gate_up, ("dp", "fsdp"), axis=0, tiled=True),
            lax.all_gather(w_down, ("dp", "fsdp"), axis=0, tiled=True),
        )
        upstream = cotangent[micro_index].astype(jnp.float32) * live_mask[:, None]
        upstream_low = upstream.astype(jnp.bfloat16)
        grad_down = trans_dot(activated, upstream_low)
        grad_activated = back_dot(upstream_low, back_down)
        (grad_both,) = swiglu_pull(grad_activated)
        grad_both_low = grad_both.astype(jnp.bfloat16)
        grad_gate_up = trans_dot(second, grad_both_low)
        grad_second = back_dot(grad_both_low, back_gate_up)
        grad_first_norm, grad_norm_two = second_norm_pull(grad_second)
        grad_first = upstream + grad_first_norm
        grad_first_low = grad_first.astype(jnp.bfloat16)
        grad_out_w = trans_dot(mixed_out, grad_first_low)
        grad_mixed = back_dot(grad_first_low, back_out)
        (
            grad_projected,
            grad_eta_linear,
            grad_eta_bias,
            grad_inner_w,
            grad_inner_b,
            grad_gain,
            grad_shift,
            grad_post_gain,
            grad_post_shift,
        ) = mixer_pull(grad_mixed)
        grad_projected_low = grad_projected.astype(jnp.bfloat16)
        grad_eta_low = grad_eta_linear.astype(jnp.bfloat16)
        grad_mixer = trans_dot(normed, grad_projected_low)
        grad_w_eta = trans_dot(normed, grad_eta_low)
        grad_normed = back_dot(grad_projected_low, back_mixer) + back_dot(grad_eta_low, back_eta)
        grad_rows, grad_norm_one = first_norm_pull(grad_normed)
        backs_list.append((grad_first + grad_rows).astype(jnp.bfloat16))
        mixer_terms = (
            grad_mixer,
            grad_w_eta,
            grad_out_w,
            grad_inner_w,
            grad_inner_b,
            grad_gain,
            grad_shift,
            grad_norm_one,
            grad_post_gain,
            grad_post_shift,
        )
        ffn_terms = (grad_gate_up, grad_down, grad_norm_two)
        reduced = reduce_all(mixer_terms, ffn_terms, grad_eta_bias)
        summed = reduced if summed is None else add_tuples(summed, reduced)
    block_out = jnp.stack(outputs_list)
    grad_tokens = jnp.stack(backs_list)
    return (
        block_out,
        grad_tokens,
        summed[0],
        summed[1],
        summed[13],
        summed[2],
        summed[3],
        summed[4],
        summed[5],
        summed[6],
        summed[7],
        summed[8],
        summed[9],
        summed[10],
        summed[11],
        summed[12],
    )


def solution(mesh):
    return jax.shard_map(
        body,
        mesh=mesh,
        in_specs=(
            P(None, ("dp", "fsdp"), None),
            P(None, ("dp", "fsdp")),
            P(None, ("dp", "fsdp"), None),
            P(("dp", "fsdp"), None),
            P(("dp", "fsdp"), None),
            P(),
            P(("dp", "fsdp"), None),
            P(("dp", "fsdp"), None),
            P(("dp", "fsdp")),
            P(("dp", "fsdp")),
            P(("dp", "fsdp")),
            P(("dp", "fsdp")),
            P(("dp", "fsdp")),
            P(("dp", "fsdp")),
            P(("dp", "fsdp"), None),
            P(("dp", "fsdp"), None),
            P(("dp", "fsdp")),
        ),
        out_specs=(
            P(None, ("dp", "fsdp"), None),
            P(None, ("dp", "fsdp"), None),
            P(("dp", "fsdp"), None),
            P(("dp", "fsdp"), None),
            P(),
            P(("dp", "fsdp"), None),
            P(("dp", "fsdp"), None),
            P(("dp", "fsdp")),
            P(("dp", "fsdp")),
            P(("dp", "fsdp")),
            P(("dp", "fsdp")),
            P(("dp", "fsdp")),
            P(("dp", "fsdp")),
            P(("dp", "fsdp"), None),
            P(("dp", "fsdp"), None),
            P(("dp", "fsdp")),
        ),
        check_vma=False,
    )
```

profile of v0, /device:TPU:0, one launch (start us, length us, event | category | flops | bytes accessed | tf_op | source)
XLA Modules:
  0.0 3191.7 jit_solution(12804347696253901364)
XLA Ops:
  10.1 71.9 %all_gather.26 = bf16[768,64]{1,0:T(8,128)(2,1)S(1)} all-gather(bf16[24,64]{1,0:T(8,128)(2,1)} %param.32), channel_id=1, replica_groups=mesh['dp'=4,'fsdp'=8] {'dp','fsdp'}, dimensions={0}, use_global_device_ids=true | all-gather | bytes 101376 | tf_op jit(solution)/shard_map/all_gather | solution.py:144
  83.8 37.3 %all-reduce.31 = (bf16[768]{0:T(1024)(128)(2,1)S(1)}, bf16[768]{0:T(1024)(128)(2,1)S(1)}, bf16[768]{0:T(1024)(128)(2,1)S(1)}, bf16[768]{0:T(1024)(128)(2,1)S(1)}...) all-reduce(bf16[768]{0:T(1024)(128)(2,1)S(1)} %dynamic-update-slice, ...), channel_id=1, replica_groups=mesh['dp'=4,'fsdp'=8] {'dp','fsdp'}, use_global_device_ids=true, to_apply=%add.14 | all-reduce | flops 5376 | bytes 21504
  126.8 67.3 %all-gather = bf16[32,24,12]{1,2,0:T(8,128)(2,1)S(1)} all-gather(bf16[1,24,12]{1,2,0:T(8,128)(2,1)S(1)} %bitcast.1084), channel_id=1, replica_groups=mesh['dp'=4,'fsdp'=8] {'dp','fsdp'}, dimensions={0}, use_global_device_ids=true | all-gather | bytes 19008 | tf_op jit(solution)/shard_map/all_gather | solution.py:142
  237.8 6.2 broadcast.1236.clone
  244.0 381.3 %while.100 = (s32[]{:T(128)}, f32[1,12,64,64]{3,2,1,0:T(8,128)S(1)}, f32[1,12,64]{2,1,0:T(8,128)S(1)}, f32[32,1,12,16,64]{4,3,2,1,0:T(8,128)}, f32[32,1,12,64,64...) while((s32[]{:T(128)}, f32[1,12,64,64]{3,2,1,0:T(8,128)S(1)}, ...), condition=%wide.region_8.9_spmd.clone.clone, body=%wide.region_1.8_spmd.clone.clone.sunk | while | flops 33646592 | bytes 3002809 | solution.py:82
  662.7 6.1 broadcast.1236.clone.1
  669.5 446.1 %while.101 = (s32[]{:T(128)}, f32[1,12,64,64]{3,2,1,0:T(8,128)S(1)}, f32[1,12,64]{2,1,0:T(8,128)S(1)}, f32[32,1,12,16,64]{4,3,2,1,0:T(8,128)}, f32[32,1,12,64,64...) while((s32[]{:T(128)}, f32[1,12,64,64]{3,2,1,0:T(8,128)S(1)}, ...), condition=%wide.region_20.21_spmd.clone.clone, body=%wide.region_13.20_spmd.clone.clone.sunk | while | flops 33646592 | bytes 3022605 | solution.py:82
  1142.8 9.1 fusion.346
  1157.8 10.4 fusion.308
  1168.3 9.3 fusion.307
  1183.4 9.7 multiply_reduce_fusion.25
  1200.5 7.3 multiply_reduce_fusion.26
  1228.0 657.9 %while.103 = (s32[]{:T(128)}, f32[12,1,64]{2,1,0:T(1,128)}, f32[12,1,64]{2,1,0:T(1,128)}, f32[1,12,64,64]{2,3,1,0:T(8,128)}, f32[1,12,64]{2,1,0:T(8,128)}, /*ind...) while((s32[]{:T(128)}, f32[12,1,64]{2,1,0:T(1,128)}, ...), condition=%wide.region_78.79_spmd.clone, body=%wide.region_55.78_spmd.clone.sunk | while | flops 91491632 | bytes 7898130 | solution.py:82
  1905.3 657.7 %while.102 = (s32[]{:T(128)}, f32[12,1,64]{2,1,0:T(1,128)}, f32[12,1,64]{2,1,0:T(1,128)}, f32[1,12,64,64]{2,3,1,0:T(8,128)}, f32[1,12,64]{2,1,0:T(8,128)}, /*ind...) while((s32[]{:T(128)}, f32[12,1,64]{2,1,0:T(1,128)}, ...), condition=%wide.region_50.51_spmd.clone, body=%wide.region_27.50_spmd.clone.sunk | while | flops 91491632 | bytes 7898130 | solution.py:82
  2637.0 6.0 fusion.347
  2643.1 8.5 convolution_add_fusion.13
  2651.7 12.2 fusion.302
  2663.9 14.2 convolution_add_fusion.12
  2684.1 6.6 fusion.349
  2701.3 38.5 %all-reduce.30 = (f32[768,12]{0,1:T(8,128)S(1)}, f32[12]{0:T(128)}, f32[768]{0:T(1024)S(1)}, f32[768]{0:T(1024)S(1)}, f32[768]{0:T(1024)S(1)}, /*index=5*/f32[76...) all-reduce(f32[768,12]{0,1:T(8,128)S(1)} %convolution_add_fusion.18, ...), channel_id=16, replica_groups=mesh['dp'=4,'fsdp'=8] {'dp','fsdp'}, use_global_device_ids=true, to_apply=%region_82.83.clone | all-reduce | flops 14604 | bytes 116832
  2755.6 6.1 reduce-scatter.11.cloned.1.call-done
  2761.8 119.9 %reduce-scatter.15.cloned.1.call-done = f32[64,768]{1,0:T(8,128)} async-done(((f32[2048,768]{1,0:T(8,128)}), f32[64,768]{1,0:T(8,128)}) %reduce-scatter.15.cloned.1.call-update) | async-done | bytes 196624 | tf_op jit(solution)/shard_map/reduce_scatter | solution.py:177
  2881.7 142.3 %reduce-scatter.9.cloned.1.call-done = f32[24,3072]{1,0:T(8,128)} async-done(((f32[768,3072]{1,0:T(8,128)}), f32[24,3072]{1,0:T(8,128)}) %reduce-scatter.9.cloned.1.call-update) | async-done | bytes 294928 | tf_op jit(solution)/shard_map/reduce_scatter | solution.py:164
  3023.9 161.0 %reduce-scatter.13.cloned.1.call-done = f32[24,4096]{1,0:T(8,128)} async-done(((f32[768,4096]{1,0:T(8,128)}), f32[24,4096]{1,0:T(8,128)}) %reduce-scatter.13.cloned.1.call-update) | async-done | bytes 393232 | tf_op jit(solution)/shard_map/reduce_scatter | solution.py:176
  (6849 shorter events, 2387.8 us)
Async XLA Ops:
  7.2 75.0 %copy-start.100 = (bf16[24]{0:T(256)(128)(2,1)S(1)}, bf16[24]{0:T(256)(128)(2,1)}, u32[]{:S(2)}) copy-start(bf16[24]{0:T(256)(128)(2,1)} %param.33) | copy-start | bytes 148
  7.2 75.2 %copy-start.101 = (bf16[24]{0:T(256)(128)(2,1)S(1)}, bf16[24]{0:T(256)(128)(2,1)}, u32[]{:S(2)}) copy-start(bf16[24]{0:T(256)(128)(2,1)} %param.36) | copy-start | bytes 148
  7.2 75.4 %copy-start.102 = (bf16[24]{0:T(256)(128)(2,1)S(1)}, bf16[24]{0:T(256)(128)(2,1)}, u32[]{:S(2)}) copy-start(bf16[24]{0:T(256)(128)(2,1)} %param.34) | copy-start | bytes 148
  7.2 75.6 %copy-start.103 = (bf16[24]{0:T(256)(128)(2,1)S(1)}, bf16[24]{0:T(256)(128)(2,1)}, u32[]{:S(2)}) copy-start(bf16[24]{0:T(256)(128)(2,1)} %param.35) | copy-start | bytes 148
  7.2 75.9 %copy-start.104 = (bf16[24]{0:T(256)(128)(2,1)S(1)}, bf16[24]{0:T(256)(128)(2,1)}, u32[]{:S(2)}) copy-start(bf16[24]{0:T(256)(128)(2,1)} %param.38) | copy-start | bytes 148
  7.2 76.1 %copy-start.105 = (bf16[24]{0:T(256)(128)(2,1)S(1)}, bf16[24]{0:T(256)(128)(2,1)}, u32[]{:S(2)}) copy-start(bf16[24]{0:T(256)(128)(2,1)} %param.37) | copy-start | bytes 148
  7.2 76.3 %copy-start.106 = (bf16[24]{0:T(256)(128)(2,1)S(1)}, bf16[24]{0:T(256)(128)(2,1)}, u32[]{:S(2)}) copy-start(bf16[24]{0:T(256)(128)(2,1)} %param.41) | copy-start | bytes 148
  7.3 113.9 %copy-start.98 = (s32[2,1]{0,1:T(1,128)S(1)}, s32[2,1]{0,1:T(1,128)}, u32[]{:S(2)}) copy-start(s32[2,1]{0,1:T(1,128)} %param.26) | copy-start | bytes 28
  7.3 119.1 %copy-start.13 = (bf16[2,512,768]{2,1,0:T(8,128)(2,1)S(1)}, bf16[2,512,768]{2,1,0:T(8,128)(2,1)}, u32[]{:S(2)}) copy-start(bf16[2,512,768]{2,1,0:T(8,128)(2,1)} %param.25) | copy-start | bytes 4718596
  7.3 192.1 %all-gather.6.cloned.1.call-start = ((), (), s32[]{:S(2)}) async-start(), calls=%async_computation.5 | async-start | bytes 4866048 | tf_op jit(solution)/shard_map/all_gather | solution.py:141
  8.0 1131.0 %all-gather.8.cloned.1.call-start = ((), (), s32[]{:S(2)}) async-start(), calls=%async_computation.6 | async-start | bytes 1216512 | tf_op jit(solution)/shard_map/all_gather | solution.py:143
  8.8 1134.0 %all-gather.10.cloned.1.call-start = ((), (), s32[]{:S(2)}) async-start(), calls=%async_computation.7 | async-start | bytes 6488064 | tf_op jit(solution)/shard_map/all_gather | solution.py:156
  9.5 1148.3 %all-gather.12.cloned.1.call-start = ((), (), s32[]{:S(2)}) async-start(), calls=%async_computation.8 | async-start | bytes 3244032 | tf_op jit(solution)/shard_map/all_gather | solution.py:157
  10.1 2745.5 %reduce-scatter.17.cloned.1.call-start = ((), (), s32[]{:S(2)}) async-start(), calls=%async_computation.13 | async-start | bytes 405504
  126.3 499.0 %copy-start.54 = (f32[768]{0:T(1024)}, f32[768]{0:T(1024)S(1)}, u32[]{:S(2)}) copy-start(f32[768]{0:T(1024)S(1)} %convert_element_type.242) | copy-start | bytes 9220
  126.7 70.0 %copy-start.85 = (f32[512]{0:T(512)}, f32[512]{0:T(512)S(1)}, u32[]{:S(2)}) copy-start(f32[512]{0:T(512)S(1)} %get-tuple-element.1448) | copy-start | bytes 6148
  126.7 71.1 %copy-start.83 = (f32[512]{0:T(512)}, f32[512]{0:T(512)S(1)}, u32[]{:S(2)}) copy-start(f32[512]{0:T(512)S(1)} %get-tuple-element.1449) | copy-start | bytes 6148
  126.8 72.6 %copy-start.88 = (f32[512]{0:T(512)}, f32[512]{0:T(512)S(1)}, u32[]{:S(2)}) copy-start(f32[512]{0:T(512)S(1)} %fusion.334) | copy-start | bytes 6148
  196.8 428.5 %copy-start.68 = (f32[512]{0:T(512)}, f32[512]{0:T(512)S(1)}, u32[]{:S(2)}) copy-start(f32[512]{0:T(512)S(1)} %fusion.336) | copy-start | bytes 6148
  669.5 446.1 %copy-start = (f32[32,1,12,16,64]{4,3,2,1,0:T(8,128)S(1)}, f32[32,1,12,16,64]{4,3,2,1,0:T(8,128)}, u32[]{:S(2)}) copy-start(f32[32,1,12,16,64]{4,3,2,1,0:T(8,128)} %get-tuple-element.996) | copy-start | bytes 4718596
  2565.2 196.6 %reduce-scatter.11.cloned.1.call-start = ((), (), s32[]{:S(2)}) async-start(), calls=%async_computation.10 | async-start | bytes 2433024 | tf_op jit(solution)/shard_map/reduce_scatter | solution.py:166
  2569.5 312.2 %reduce-scatter.15.cloned.1.call-start = ((), (), s32[]{:S(2)}) async-start(), calls=%async_computation.12 | async-start | bytes 6488064 | tf_op jit(solution)/shard_map/reduce_scatter | solution.py:177
  2578.9 445.0 %reduce-scatter.9.cloned.1.call-start = ((), (), s32[]{:S(2)}) async-start(), calls=%async_computation.9 | async-start | bytes 9732096 | tf_op jit(solution)/shard_map/reduce_scatter | solution.py:164
  2651.6 533.3 %reduce-scatter.13.cloned.1.call-start = ((), (), s32[]{:S(2)}) async-start(), calls=%async_computation.11 | async-start | bytes 12976128 | tf_op jit(solution)/shard_map/reduce_scatter | solution.py:176
  (623 other events, 3195.5 us)
Sparse Core Ops, SparseCore 0:
  11.0 67.0 all-gather.5
  81.0 53.1 all-gather.7
  137.2 68.5 all-gather.9
  208.5 57.6 all-gather.11
  2565.3 91.8 reduce-scatter.16
  2663.8 97.9 reduce-scatter.10
  2768.0 113.6 reduce-scatter.14
  2889.1 134.7 reduce-scatter.8
  3030.5 154.3 reduce-scatter.12
where the time goes:
time: 3220 us; the launch traced here: 3190 us
  matrix products  1220 us (38%)
  local copies, waits for them, and re-layouts  715 us (22%)
  other arithmetic  552 us (17%)
  waiting for transfers between devices  432 us (13%)
  blocking collectives  215 us (7%)
  loops' own time  38.6 us (1%)
    dot_general x256, matrix products, inner_step(): jnp.einsum('ghme,ghef->ghmf', queries, weight, precision=highest)  313 us
    squeeze x320, local copies, waits for them, and re-layouts, inner_layer(): lax.scan(stepper, start, (split_heads(queries), split_heads(key_rows), sp...  281 us
    dot_general x256, matrix products, inner_step(): jnp.einsum('ghme,ghef->ghmf', key_rows, weight, precision=highest)  274 us
    dot_general x192, matrix products, inner_step(): jnp.einsum('ghme,ghmf->ghef', key_rows * last_row[..., None], inner_grad,...  201 us
    reduce_scatter x1, waiting for transfers between devices, reduce_all(): lax.psum_scatter(ffn_terms[0], ('dp', 'fsdp'), scatter_dimension=0, tiled...  161 us
    dynamic_update_slice x128, other arithmetic, inner_layer(): lax.scan(stepper, start, (split_heads(queries), split_heads(key_rows), sp...  160 us
    reduce_scatter x1, waiting for transfers between devices, reduce_all(): lax.psum_scatter(mixer_terms[0], ('dp', 'fsdp'), scatter_dimension=0, til...  142 us
    dot_general x256, matrix products, inner_step(): scores = jnp.einsum('ghme,ghne->ghmn', queries, key_rows, precision=highest)  141 us

commit v1 on v0

v1 whole, which is shorter than its diff:
```python
import jax
import jax.numpy as jnp
from jax import lax
from jax.experimental import pallas as pl
from jax.experimental.pallas import tpu as pltpu
from jax.sharding import PartitionSpec as P
import numpy as np

MINI = 16
HEAD = 64
PAIR = 2 * HEAD
epsilon = 1e-06
low = jnp.bfloat16
full = jnp.float32


def dot_nn(former, latter):
    return lax.dot_general(former, latter, (((1,), (0,)), ((), ())), preferred_element_type=full)


def dot_nt(former, latter):
    return lax.dot_general(former, latter, (((1,), (1,)), ((), ())), preferred_element_type=full)


def tile_of(rows, at):
    return rows[:, PAIR * at : PAIR * (at + 1)]


def expand(rows, sides):
    count = rows.shape[1] // PAIR
    zero = jnp.zeros((MINI, PAIR), rows.dtype)
    blocks = []
    for side in range(2):
        for at in range(count):
            kept = tile_of(rows, at) * sides[side]
            blocks.append(jnp.concatenate([kept if other == at else zero for other in range(count)], axis=1))
    return jnp.concatenate(blocks, axis=0)


def to_feature(rows, left):
    count = rows.shape[1] // PAIR
    stacked = jnp.concatenate([tile_of(rows, at) for at in range(count)] * 2, axis=0).T
    return jnp.where(left[:HEAD], stacked[:HEAD], stacked[HEAD:])


def to_rows(columns, left):
    turned = jnp.concatenate([columns, columns], axis=0).T
    count = 4
    return jnp.concatenate(
        [
            jnp.where(left[:MINI], turned[MINI * at : MINI * (at + 1)], turned[HEAD + MINI * at : HEAD + MINI * (at + 1)])
            for at in range(count)
        ],
        axis=1,
    )


def mean_rows(values):
    return jnp.sum(values, axis=0, keepdims=True) * (1.0 / values.shape[0])


def both_sequences(ref, rows, base, width):
    return jnp.concatenate([ref[0, rows, base : base + width], ref[1, rows, base : base + width]], axis=1)


def store_sequences(ref, rows, base, width, pieces, kind):
    whole = jnp.concatenate(pieces, axis=1)
    ref[0, rows, base : base + width] = whole[:, :width].astype(kind)
    ref[1, rows, base : base + width] = whole[:, width:].astype(kind)


def ttt_forward_kernel(steps, q_ref, k_ref, v_ref, rate_ref, w0_ref, b0_ref, gain_ref, shift_ref, sides_ref, tri_ref, ones_ref,
                       *outs):
    out_ref, w_ref, xh_ref, h_ref, grs_ref, xb_ref, stat_ref, score_ref, w_run, b_run = outs[-10:]
    width = 768

    @pl.when(pl.program_id(0) == 0)
    def _():
        w_run[...] = w0_ref[...]
        b_run[...] = b0_ref[...]

    sides = [sides_ref[0:MINI], sides_ref[MINI : 2 * MINI]]
    left = lax.broadcasted_iota(jnp.int32, (HEAD, PAIR), 1) < HEAD
    tri = tri_ref[0:MINI]
    same_head = ones_ref[...]

    def one(at, carry):
        rows = pl.ds(at * MINI, MINI)
        queries = both_sequences(q_ref, rows, 0, width)
        keys = both_sequences(k_ref, rows, 0, width)
        targets = both_sequences(v_ref, rows, 0, width) - keys
        results = []
        for part in range(3):
            wide = slice(4 * PAIR * part, 4 * PAIR * (part + 1))
            thin = slice(PAIR * part, PAIR * (part + 1))
            gains, shifts = gain_ref[:, thin], shift_ref[:, thin]
            rate = rate_ref[at, :, thin]
            weight, offset = w_run[:, wide], b_run[:, thin]
            weight_low = weight.astype(low)
            w_ref[at, :, wide] = weight_low
            query_low, key_low = queries[:, wide].astype(low), keys[:, wide].astype(low)
            key_block, query_block = expand(key_low, sides), expand(query_low, sides)
            both = dot_nt(weight_low, jnp.concatenate([key_block, query_block], axis=0))
            hidden = both[:, :PAIR] + offset
            centred = hidden - mean_rows(hidden)
            inverse = lax.rsqrt(mean_rows(centred * centred) + epsilon)
            normed = centred * inverse
            target = to_feature(targets[:, wide], left)
            held = gains * normed + shifts - target
            residual = held * gains
            residual_mean = mean_rows(residual)
            cross = mean_rows(residual * normed)
            inner_grad = (residual - residual_mean - normed * cross) * inverse
            scaled = inner_grad * (rate * (1.0 / MINI))
            scaled_low = scaled.astype(low)
            w_run[:, wide] = weight - dot_nn(scaled_low, key_block)
            b_run[:, thin] = offset - dot_nn(scaled_low, same_head)
            scores = dot_nt(query_low, key_block) + 1.0
            mixing = (tri * rate * scores).astype(low)
            mixing_block = jnp.concatenate([mixing] * 8, axis=0) * same_head
            updated = both[:, PAIR:] + offset - dot_nt(inner_grad.astype(low), mixing_block)
            updated = updated - mean_rows(updated)
            updated_inverse = lax.rsqrt(mean_rows(updated * updated) + epsilon)
            updated = updated * updated_inverse
            results.append(to_rows(updated * gains + shifts, left))
            xh_ref[at, :, thin] = normed
            h_ref[at, :, thin] = held
            grs_ref[at, :, thin] = scaled
            xb_ref[at, :, thin] = updated
            stat_ref[at, 0:1, thin] = inverse
            stat_ref[at, 1:2, thin] = residual_mean
            stat_ref[at, 2:3, thin] = cross
            stat_ref[at, 3:4, thin] = updated_inverse
            score_ref[at, :, thin] = scores
        result = queries + jnp.concatenate(results, axis=1)
        out_ref[0, rows, :] = result[:, :width]
        out_ref[1, rows, :] = result[:, width:]
        return carry

    lax.fori_loop(0, steps, one, 0)


def ttt_backward_kernel(steps, q_ref, k_ref, dout_ref, rate_ref, w_ref, xh_ref, h_ref, grs_ref, xb_ref, stat_ref, score_ref,
                        gain_ref, sides_ref, tri_ref, ones_ref, dw_in, db_in, dgain_in, dshift_in, *outs):
    grad_ref, rdr_ref, dw_ref, db_ref, dgain_ref, dshift_ref = outs[-6:]
    width = 768

    @pl.when(pl.program_id(0) == 0)
    def _():
        dw_ref[...] = dw_in[...]
        db_ref[...] = db_in[...]
        dgain_ref[...] = dgain_in[...]
        dshift_ref[...] = dshift_in[...]

    sides = [sides_ref[0:MINI], sides_ref[MINI : 2 * MINI]]
    wide_sides = [jnp.concatenate([side] * 4, axis=0) for side in sides]
    left = lax.broadcasted_iota(jnp.int32, (HEAD, PAIR), 1) < HEAD
    tri = tri_ref[0:MINI]
    tri_turned = tri_ref[MINI : 2 * MINI]
    same_head = ones_ref[...]

    def block_of(weight):
        return jnp.concatenate([weight * wide_sides[0], weight * wide_sides[1]], axis=0)

    def one(step, carry):
        at = steps - 1 - step
        rows = pl.ds(at * MINI, MINI)
        queries = both_sequences(q_ref, rows, 0, width)
        keys = both_sequences(k_ref, rows, 0, width)
        douts = both_sequences(dout_ref, rows, 0, width)
        query_grads, key_grads, value_grads = [], [], []
        for part in range(3):
            wide = slice(4 * PAIR * part, 4 * PAIR * (part + 1))
            thin = slice(PAIR * part, PAIR * (part + 1))
            gains = gain_ref[:, thin]
            rate = rate_ref[at, :, thin]
            normed, held, scaled, updated = xh_ref[at, :, thin], h_ref[at, :, thin], grs_ref[at, :, thin], xb_ref[at, :, thin]
            inverse, residual_mean, cross, updated_inverse = (stat_ref[at, row : row + 1, thin] for row in range(4))
            scores = score_ref[at, :, thin]
            weight_low = w_ref[at, :, wide]
            dweight, doffset = dw_ref[:, wide], db_ref[:, thin]
            dweight_low = dweight.astype(low)
            query_low, key_low = queries[:, wide].astype(low), keys[:, wide].astype(low)
            key_block, query_block = expand(key_low, sides), expand(query_low, sides)
            mixing = (tri * rate * scores).astype(low)
            mixing_block = jnp.concatenate([mixing] * 8, axis=0) * same_head

            dout = to_feature(douts[:, wide], left)
            dupdated = dout * gains
            dupdated = updated_inverse * (dupdated - mean_rows(dupdated) - updated * mean_rows(dupdated * updated))
            dupdated_low = dupdated.astype(low)
            key_dw = dot_nt(dweight_low, key_block) + doffset
            grad_in = -dot_nn(dupdated_low, mixing_block) - (rate * (1.0 / MINI)) * key_dw
            rate_part = -jnp.sum(scaled * key_dw, axis=0, keepdims=True)
            residual = held * gains
            in_mean = mean_rows(grad_in)
            in_cross = mean_rows(grad_in * normed)
            in_held = inverse * (mean_rows(grad_in * residual) - residual_mean * in_mean - cross * in_cross)
            dresidual = inverse * (grad_in - in_mean - normed * in_cross)
            dtarget = dresidual * gains
            dnormed = dtarget * gains - inverse * (grad_in * cross + in_cross * residual)
            dhidden = inverse * (dnormed - mean_rows(dnormed) - normed * (mean_rows(dnormed * normed) + in_held))
            dhidden_low = dhidden.astype(low)
            dgain_ref[:, thin] += dout * updated + dresidual * (held + gains * normed)
            dshift_ref[:, thin] += dout + dtarget
            db_ref[:, thin] = doffset + dot_nn((dupdated + dhidden).astype(low), same_head)
            dw_ref[:, wide] = dweight + dot_nn(
                jnp.concatenate([dupdated_low, dhidden_low], axis=1), jnp.concatenate([query_block, key_block], axis=0)
            )
            dupdated_rows = to_rows(dupdated, left).astype(low)
            dhidden_rows = to_rows(dhidden, left).astype(low)
            scaled_rows = to_rows(-scaled, left).astype(low)
            dtarget_rows = to_rows(dtarget, left)
            dmix = dot_nt(dupdated_rows, expand(scaled_rows, sides)) * tri * MINI
            dmix_turned = dot_nt(scaled_rows, expand(dupdated_rows, sides)) * tri_turned * MINI
            rdr_ref[at, :, thin] = rate_part + jnp.sum(dmix * scores, axis=0, keepdims=True)
            dmix_low, dmix_turned_low = dmix.astype(low), dmix_turned.astype(low)
            for tile in range(4):
                block = block_of(tile_of(weight_low, tile))
                dblock = block_of(tile_of(dweight_low, tile))
                query_grads.append(
                    tile_of(douts[:, wide], tile)
                    + dot_nn(
                        jnp.concatenate([tile_of(dupdated_rows, tile), dmix_low], axis=1),
                        jnp.concatenate([block, tile_of(key_block, tile)], axis=0),
                    )
                )
                key_grads.append(
                    tile_of(dtarget_rows, tile)
                    + dot_nn(
                        jnp.concatenate([tile_of(dhidden_rows, tile), tile_of(scaled_rows, tile), dmix_turned_low], axis=1),
                        jnp.concatenate([block, dblock, tile_of(query_block, tile)], axis=0),
                    )
                )
                value_grads.append(-tile_of(dtarget_rows, tile))
        store_sequences(grad_ref, rows, 0, width, query_grads, low)
        store_sequences(grad_ref, rows, width, width, key_grads, low)
        store_sequences(grad_ref, rows, 2 * width, width, value_grads, low)
        return carry

    lax.fori_loop(0, steps, one, 0)


def ttt_constants():
    lane = np.arange(PAIR)
    row = np.arange(MINI)
    sides = np.concatenate([np.tile(lane < HEAD, (MINI, 1)), np.tile(lane >= HEAD, (MINI, 1))]).astype(np.float32)
    col = lane % MINI
    tri = np.where(col[None] <= row[:, None], 1.0 / (row[:, None] + 1.0), 0.0)
    tri_turned = np.where(row[:, None] <= col[None], 1.0 / (col[None] + 1.0), 0.0)
    ones = (lane[:, None] // MINI == lane[None] // MINI).astype(np.float32)
    return (
        jnp.asarray(sides, low),
        jnp.asarray(np.concatenate([tri, tri_turned]), full),
        jnp.asarray(ones, low),
    )


def spec(shape, index):
    return pl.BlockSpec(shape, index)


def ttt_forward(projected, rates, state, gains, shifts, steps=4):
    count = projected.shape[1] // MINI
    first, begin, end, before = 0, 0, count, None
    queries, keys, values = projected, projected, projected
    sides, tri, ones = ttt_constants()
    whole = lambda *shape: pl.BlockSpec(shape, lambda at: (0,) * len(shape))
    column = lambda place: pl.BlockSpec((2, steps * MINI, 768), lambda at, place=place: (0, first + at, place))
    part = column(0)
    saved = lambda *tail: pl.BlockSpec((steps,) + tail, lambda at: (at, 0, 0))
    made = lambda kind, *tail: jax.ShapeDtypeStruct((end - begin,) + tail, kind)
    extra = [] if before is None else [before]
    inputs = [queries, keys, values, rates, *state, gains, shifts, sides, tri, ones]
    out, *rest = pl.pallas_call(
        lambda *refs: ttt_forward_kernel(steps, *refs),
        grid=((end - begin) // steps,),
        in_specs=[column(0), column(1), column(2), pl.BlockSpec((steps, 1, 384), lambda at: (first + at, 0, 0)), whole(64, 1536), whole(64, 384),
                  whole(64, 384), whole(64, 384), whole(32, 128), whole(32, 128), whole(128, 128)]
        + [pl.BlockSpec(memory_space=pl.ANY)] * len(extra),
        out_specs=[part, saved(64, 1536), saved(64, 384), saved(64, 384), saved(64, 384), saved(64, 384), saved(8, 384),
                   saved(16, 384), whole(64, 1536), whole(64, 384)],
        out_shape=[jax.ShapeDtypeStruct((2, count * MINI, 768), full), made(low, 64, 1536), made(full, 64, 384), made(full, 64, 384),
                   made(full, 64, 384), made(full, 64, 384), made(full, 8, 384), made(full, 16, 384),
                   jax.ShapeDtypeStruct((64, 1536), full), jax.ShapeDtypeStruct((64, 384), full)],
        input_output_aliases={len(inputs): 0} if extra else {},
        compiler_params=pltpu.CompilerParams(vmem_limit_bytes=40 * 1024 * 1024),
        cost_estimate=pl.CostEstimate(flops=(end - begin) * 1_400_000_000, bytes_accessed=(end - begin) * 1_500_000, transcendentals=0),
        name="ttt_forward",
    )(*inputs, *extra)
    return out, rest[:7], rest[7:]


def ttt_backward(projected, dout, rates, saved_arrays, state, gains, begin, end, before, steps=4):
    count = projected.shape[1] // MINI
    first, blocks = begin // steps, (end - begin) // steps
    queries, keys = projected, projected
    sides, tri, ones = ttt_constants()
    whole = lambda *shape: pl.BlockSpec(shape, lambda at: (0,) * len(shape))
    part = lambda width, place=0: pl.BlockSpec((2, steps * MINI, width), lambda at: (0, first + blocks - 1 - at, place))
    saved = lambda *tail: pl.BlockSpec((steps,) + tail, lambda at: (first + blocks - 1 - at, 0, 0))
    made = lambda *tail: pl.BlockSpec((steps,) + tail, lambda at: (blocks - 1 - at, 0, 0))
    extra = [] if before is None else [before]
    inputs = [queries, keys, dout, rates, *saved_arrays, gains, sides, tri, ones, *state]
    states = [whole(64, 1536), whole(64, 384), whole(64, 384), whole(64, 384)]
    grad, rate_back, *state = pl.pallas_call(
        lambda *refs: ttt_backward_kernel(steps, *refs),
        grid=(blocks,),
        in_specs=[part(768), part(768, 1), part(768), saved(1, 384),
                  saved(64, 1536), saved(64, 384), saved(64, 384), saved(64, 384), saved(64, 384), saved(8, 384), saved(16, 384),
                  whole(64, 384), whole(32, 128), whole(32, 128), whole(128, 128)]
        + states + [pl.BlockSpec(memory_space=pl.ANY)] * len(extra),
        out_specs=[part(2304), made(1, 384)] + states,
        out_shape=[jax.ShapeDtypeStruct((2, count * MINI, 2304), low), jax.ShapeDtypeStruct((end - begin, 1, 384), full)]
        + [jax.ShapeDtypeStruct((64, 1536), full)] + [jax.ShapeDtypeStruct((64, 384), full)] * 3,
        input_output_aliases={len(inputs): 0} if extra else {},
        compiler_params=pltpu.CompilerParams(vmem_limit_bytes=40 * 1024 * 1024),
        cost_estimate=pl.CostEstimate(flops=(end - begin) * 2_000_000_000, bytes_accessed=(end - begin) * 1_500_000, transcendentals=0),
        name="ttt_backward",
    )(*inputs, *extra)
    return grad, rate_back, state


def silu_parts(gate):
    sigma = jax.nn.sigmoid(gate)
    return gate * sigma, sigma * (1.0 + gate * (1.0 - sigma))


def gelu_parts(values):
    slope = 0.7978845608028654
    turn = jnp.tanh(slope * (values + 0.044715 * values * values * values))
    half = 0.5 * (1.0 + turn)
    return values * half, half + 0.5 * values * (1.0 - turn * turn) * slope * (1.0 + 3 * 0.044715 * values * values)


def row_mean(values):
    return jnp.mean(values, axis=-1, keepdims=True)


def dot_tn(former, latter):
    return lax.dot_general(former, latter, (((0,), (0,)), ((), ())), preferred_element_type=full)


def exact_dot(former, latter):
    total = None
    for _ in range(3):
        part = former.astype(low)
        former = former - part.astype(full)
        term = dot_nn(part, latter)
        total = term if total is None else total + term
    return total


def constant_spec(*shape, at=0, buffers=None):
    index = lambda *steps: (0,) * (len(shape) - 1) + (at,)
    if buffers is None:
        return pl.BlockSpec(shape, index)
    return pl.BlockSpec(shape, index, pipeline_mode=pl.Buffered(buffers))


def call(kernel, name, grid, prefetch, in_specs, out_specs, out_shape, scratch, cost, arrays):
    return pl.pallas_call(
        kernel,
        grid_spec=pltpu.PrefetchScalarGridSpec(
            num_scalar_prefetch=prefetch, grid=grid, in_specs=in_specs, out_specs=out_specs, scratch_shapes=scratch
        ),
        out_shape=out_shape,
        compiler_params=pltpu.CompilerParams(vmem_limit_bytes=56 * 1024 * 1024),
        cost_estimate=pl.CostEstimate(flops=cost, bytes_accessed=cost // 500, transcendentals=0),
        name=name,
    )(*arrays)


ETA = 64
VECTORS = 80
BIAS = 96


def lane_table():
    lane = np.arange(384)
    part, side, tile, token = lane // 128, lane // 64 % 2, lane // 16 % 4, lane % 16
    pair = 4 * part + tile
    return token, pair // 6, 2 * (pair % 6) + side


def lane_constants():
    token, sequence, head = lane_table()
    table = np.zeros((32, 384), np.float32)
    table[:MINI] = token[None] == np.arange(MINI)[:, None]
    table[16], table[17] = sequence, token
    chosen = np.zeros((PAIR, 384), np.float32)
    chosen[ETA + head, np.arange(384)] = 1
    return jnp.asarray(table), jnp.asarray(chosen, low)


def project_kernel(length_ref, tokens_ref, w_ref, bias_ref, table_ref, chosen_ref,
                   proj_ref, normed_ref, rate_ref, rest_ref, wt_ref, b_ref, gain_ref, shift_ref, vec_ref):
    at = pl.program_id(0)
    wide = w_ref.shape[1] - PAIR

    @pl.when(at == 0)
    def _():
        small = w_ref[:, wide:].astype(full)
        turned = small.T
        wt_ref[:, :768] = turned[:HEAD]
        wt_ref[:, 768:] = turned[:HEAD]
        vec_ref[...] = turned[VECTORS : VECTORS + 8]
        for place, ref in enumerate((b_ref, gain_ref, shift_ref)):
            total = jnp.zeros((HEAD, 384), full)
            for head in range(12):
                column = small[HEAD * head : HEAD * (head + 1), VECTORS + place : VECTORS + place + 1]
                total = total + column * chosen_ref[ETA + head : ETA + head + 1].astype(full)
            ref[...] = total
        rate_ref[...] = jnp.zeros_like(rate_ref)
        rest_ref[...] = jnp.zeros_like(rest_ref)

    values = tokens_ref[...].astype(full)
    normed = (values * lax.rsqrt(row_mean(values * values) + epsilon) * vec_ref[3:4]).astype(low)
    normed_ref[...] = normed
    proj_ref[:, :wide] = dot_nn(normed, w_ref[:, :wide])
    last = dot_nn(normed, w_ref[:, wide:])
    proj_ref[:, wide:] = last
    spread = exact_dot(last + bias_ref[...], chosen_ref[...])
    blocks = spread.shape[0] // MINI
    spread = jnp.sum(spread.reshape(blocks, MINI, 384) * table_ref[:MINI][None], axis=1)
    sequence, token = table_ref[16:17], table_ref[17:18]
    mine = sequence == (at // 2).astype(full)
    sigma = jax.nn.sigmoid(spread)
    begin = (at % 2) * blocks
    block = lax.broadcasted_iota(jnp.int32, spread.shape, 0) + begin
    live = (block * MINI).astype(full) + token < length_ref[at // 2].astype(full)
    here = pl.ds(begin, blocks)
    rate_ref[here, 0, :] += jnp.where(live & mine, sigma * (1.0 / HEAD), 0.0)
    rest_ref[here, :] += jnp.where(mine, 1.0 - sigma, 0.0)


def project(lengths, tokens, whole, bias_row):
    rows, width = tokens.shape
    table, chosen = lane_constants()
    tile = rows // 4
    columns = whole.shape[1]
    row = lambda n: pl.BlockSpec((tile, n), lambda at, *_: (at, 0))
    shape = jax.ShapeDtypeStruct
    return call(
        project_kernel, "project", (4,), 1,
        [row(width), constant_spec(width, columns, buffers=1), constant_spec(1, PAIR), constant_spec(32, 384), constant_spec(PAIR, 384)],
        [row(columns), row(width), constant_spec(32, 1, 384), constant_spec(32, 384), constant_spec(64, 1536)]
        + [constant_spec(64, 384)] * 3 + [constant_spec(8, width)],
        [shape((rows, columns), full), shape((rows, width), low), shape((32, 1, 384), full), shape((32, 384), full),
         shape((64, 1536), full)] + [shape((64, 384), full)] * 3 + [shape((8, width), full)],
        [], 5_000_000_000, (lengths, tokens, whole, bias_row, table, chosen),
    )


def post_kernel(inner_ref, normed_ref, tokens_ref, w_gate_ref, w_out_ref, vec_ref, gate_ref, mixed_ref, first_ref, second_ref):
    gate = dot_nn(normed_ref[...], w_gate_ref[...])
    gate_ref[...] = gate
    inner = inner_ref[...]
    centred = inner - row_mean(inner)
    standard = centred * lax.rsqrt(row_mean(centred * centred) + epsilon)
    mixed = ((standard * vec_ref[4:5] + vec_ref[5:6]) * gelu_parts(gate)[0]).astype(low)
    mixed_ref[...] = mixed
    first = tokens_ref[...].astype(full) + dot_nn(mixed, w_out_ref[...])
    first_ref[...] = first
    second_ref[...] = (first * lax.rsqrt(row_mean(first * first) + epsilon) * vec_ref[6:7]).astype(low)


def post(inner, normed, tokens, fetched, vectors):
    rows, width = tokens.shape
    tile = rows // 4
    row = pl.BlockSpec((tile, width), lambda at: (at, 0))
    shape = jax.ShapeDtypeStruct
    return call(
        post_kernel, "post", (4,), 0,
        [row, row, row, constant_spec(width, width, at=0, buffers=1), constant_spec(width, width, at=1, buffers=1), constant_spec(8, width)],
        [row] * 4, [shape((rows, width), kind) for kind in (full, low, full, low)], [], 4_000_000_000,
        (inner, normed, tokens, fetched, fetched, vectors),
    )


def store_blocks(table_ref, out_ref, held_ref, block, first=0):
    if block % 8:
        out_ref[...] = held_ref[...].astype(out_ref.dtype)
        return
    for pair in range(held_ref.shape[0] // (2 * block)):
        rows = [held_ref[pl.ds(pl.multiple_of(table_ref[2 * pair + side] * block, 8), block), :] for side in range(2)]
        out_ref[2 * block * pair : 2 * block * (pair + 1), :] = jnp.concatenate(rows, axis=0).astype(out_ref.dtype)


def ffn_kernel(block, down_block, table_ref, place_ref, second_ref, first_ref, up_ref, w_gate_ref, w_up_ref, w_down_ref,
               out_ref, dsecond_ref, dboth_ref, ddown_ref, turned, total, act, both_low, held):
    at = pl.program_id(0)
    rows = second_ref.shape[0]
    tile = 256

    @pl.when(at == 0)
    def _():
        turned[...] = second_ref[...].T
        total[...] = first_ref[...]
        dsecond_ref[...] = jnp.zeros_like(dsecond_ref)

    w_gate, w_up, w_down = w_gate_ref[...], w_up_ref[...], w_down_ref[...]

    def one(place, carry):
        here = pl.ds(place * tile, tile)
        second, upstream = second_ref[here, :], up_ref[here, :]
        gate, up = dot_nn(second, w_gate), dot_nn(second, w_up)
        value, slope = silu_parts(gate)
        activated = (value * up).astype(low)
        act[here, :] = activated
        total[here, :] += dot_nn(activated, w_down)
        dact = dot_nt(upstream, w_down)
        dgate, dup = (dact * up * slope).astype(low), (dact * value).astype(low)
        both_low[here, : dgate.shape[1]] = dgate
        both_low[here, dgate.shape[1] :] = dup
        dsecond_ref[here, :] += dot_nt(dgate, w_gate) + dot_nt(dup, w_up)
        return carry

    lax.fori_loop(0, rows // tile, one, 0)
    held[...] = dot_nn(turned[...], both_low[...])
    store_blocks(table_ref, dboth_ref, held, block)
    ddown = dot_tn(act[...], up_ref[...]).astype(low)
    count = ddown.shape[0] // down_block
    for place in range(count):
        to = pl.multiple_of(place_ref[at * count + place] * down_block, 16)
        ddown_ref[pl.ds(to, down_block), :] = ddown[down_block * place : down_block * (place + 1)]

    @pl.when(at == pl.num_programs(0) - 1)
    def _():
        out_ref[...] = total[...].astype(low)


def ffn(table, inverse, second, first, upstream, fetched, w_down, devices, steps):
    rows, width = second.shape
    hidden = w_down.shape[0]
    size = hidden // steps
    begin = 2 * width // size
    shape = jax.ShapeDtypeStruct
    column = lambda first: pl.BlockSpec((width, size), lambda at, *_, first=first: (0, first + at))
    return call(
        lambda *refs: ffn_kernel(width // devices, hidden // devices, *refs), "ffn", (steps,), 2,
        [constant_spec(rows, width, buffers=1)] * 3 + [column(begin), column(begin + steps),
         pl.BlockSpec((size, width), lambda at, *_: (at, 0))],
        [constant_spec(rows, width, buffers=1), constant_spec(rows, width, buffers=1),
         pl.BlockSpec((width, 2 * size), lambda at, *_: (0, at)), constant_spec(hidden, width, buffers=1)],
        [shape((rows, width), low), shape((rows, width), full), shape((width, 2 * hidden), low), shape((hidden, width), low)],
        [pltpu.VMEM((width, rows), low), pltpu.VMEM((rows, width), full), pltpu.VMEM((rows, size), low),
         pltpu.VMEM((rows, 2 * size), low), pltpu.VMEM((width, 2 * size), full)],
        29_000_000_000, (table, inverse, second, first, upstream, fetched, fetched, w_down),
    )


def post_back_kernel(block, table_ref, dsecond_ref, first_ref, up_ref, inner_ref, gate_ref, mixed_ref, normed_ref, w_out_ref, vec_ref,
                     dfirst_ref, dgate_ref, dinner_ref, sums_ref, dout_ref, held):
    at = pl.program_id(0)

    @pl.when(at == 0)
    def _():
        sums_ref[...] = jnp.zeros_like(sums_ref)
        held[...] = jnp.zeros_like(held)

    width = first_ref.shape[1]
    first, dsecond = first_ref[...], dsecond_ref[...]
    scale = lax.rsqrt(row_mean(first * first) + epsilon)
    two_sum = jnp.sum(dsecond * first * scale, axis=0, keepdims=True)
    dsecond = dsecond * vec_ref[6:7]
    dfirst = up_ref[...].astype(full) + scale * dsecond - first * (scale * scale * scale * row_mean(first * dsecond))
    dfirst_ref[...] = dfirst
    dfirst_low = dfirst.astype(low)
    held[:, :width] += dot_tn(mixed_ref[...], dfirst_low)
    dmixed = dot_nt(dfirst_low, w_out_ref[...])
    inner = inner_ref[...]
    centred = inner - row_mean(inner)
    inverse = lax.rsqrt(row_mean(centred * centred) + epsilon)
    standard = centred * inverse
    value, slope = gelu_parts(gate_ref[...])
    dgate = (dmixed * (standard * vec_ref[4:5] + vec_ref[5:6]) * slope).astype(low)
    dgate_ref[...] = dgate
    held[:, width:] += dot_tn(normed_ref[...], dgate)
    dpost = dmixed * value
    sums_ref[4:5] += jnp.sum(dpost * standard, axis=0, keepdims=True)
    sums_ref[5:6] += jnp.sum(dpost, axis=0, keepdims=True)
    sums_ref[6:7] += two_sum
    dpost = dpost * vec_ref[4:5]
    dinner_ref[...] = inverse * (dpost - row_mean(dpost) - standard * row_mean(dpost * standard))

    @pl.when(at == pl.num_programs(0) - 1)
    def _():
        store_blocks(table_ref, dout_ref, held, block)


def post_back(table, dsecond, first, upstream, inner, gate, mixed, normed, fetched, vectors, devices):
    rows, width = first.shape
    tile = rows // 4
    row = pl.BlockSpec((tile, width), lambda at, *_: (at, 0))
    shape = jax.ShapeDtypeStruct
    return call(
        lambda *refs: post_back_kernel(width // devices, *refs), "post_back", (4,), 1,
        [row] * 7 + [constant_spec(width, width, at=1, buffers=1), constant_spec(8, width)],
        [row, row, row, constant_spec(8, width), constant_spec(width, 2 * width, buffers=1)],
        [shape((rows, width), full), shape((rows, width), low), shape((rows, width), full), shape((8, width), full),
         shape((width, 2 * width), low)],
        [pltpu.VMEM((width, 2 * width), full)], 5_000_000_000,
        (table, dsecond, first, upstream, inner, gate, mixed, normed, fetched, vectors),
    )


def weight_kernel(block, table_ref, normed_ref, grad_ref, out_ref, turned, held):
    @pl.when(pl.program_id(0) == 0)
    def _():
        turned[...] = normed_ref[...].T

    held[...] = dot_nn(turned[...], grad_ref[...])
    store_blocks(table_ref, out_ref, held, block)


def weight_grads(table, normed, grads, devices):
    rows, width = normed.shape
    columns = grads.shape[1]
    size = 384
    shape = jax.ShapeDtypeStruct
    return call(
        lambda *refs: weight_kernel(width // devices, *refs), "weight_grads", (columns // size,), 1,
        [constant_spec(rows, width, buffers=1), pl.BlockSpec((rows, size), lambda at, *_: (0, at))],
        pl.BlockSpec((width, size), lambda at, *_: (0, at)), shape((width, columns), low),
        [pltpu.VMEM((width, rows), low), pltpu.VMEM((width, size), full)], 4_000_000_000, (table, normed, grads),
    )


def finish_kernel(tokens_ref, dfirst_ref, dqkv_ref, dgate_ref, rate_ref, rest_ref, w_ref, w_gate_ref, vec_ref, table_ref, chosen_ref,
                  out_ref, dlog_ref, sums_ref):
    at = pl.program_id(0)
    wide = dqkv_ref.shape[1]

    @pl.when(at == 0)
    def _():
        sums_ref[...] = jnp.zeros_like(sums_ref)

    blocks = tokens_ref.shape[0] // MINI
    here = pl.ds((at % 2) * blocks, blocks)
    mine = (table_ref[16:17] == (at // 2).astype(full)).astype(full)
    dlog = rate_ref[here, 0, :] * rest_ref[here, :] * mine
    dlog = (dlog[:, None, :] * table_ref[:MINI][None]).reshape(blocks * MINI, 384).astype(low)
    dlog = dot_nt(dlog, chosen_ref[...]).astype(low)
    dlog_ref[...] = dlog
    dnormed = dot_nt(dqkv_ref[...], w_ref[:, :wide]) + dot_nt(dgate_ref[...], w_gate_ref[...]) + dot_nt(dlog, w_ref[:, wide:])
    values = tokens_ref[...].astype(full)
    scale = lax.rsqrt(row_mean(values * values) + epsilon)
    sums_ref[3:4] += jnp.sum(dnormed * values * scale, axis=0, keepdims=True)
    dnormed = dnormed * vec_ref[3:4]
    back = scale * dnormed - values * (scale * scale * scale * row_mean(values * dnormed))
    out_ref[...] = (dfirst_ref[...] + back).astype(low)


def finish(tokens, dfirst, dqkv, dgate, rate_back, rest, whole, fetched, vectors):
    rows, width = tokens.shape
    tile = rows // 4
    table, chosen = lane_constants()
    row = lambda n: pl.BlockSpec((tile, n), lambda at: (at, 0))
    shape = jax.ShapeDtypeStruct
    return call(
        finish_kernel, "finish", (4,), 0,
        [row(width), row(width), row(3 * width), row(width), constant_spec(32, 1, 384), constant_spec(32, 384),
         constant_spec(width, whole.shape[1], buffers=1), constant_spec(width, width, at=0, buffers=1), constant_spec(8, width),
         constant_spec(32, 384), constant_spec(PAIR, 384)],
        [row(width), row(PAIR), constant_spec(8, width)],
        [shape((rows, width), low), shape((rows, PAIR), low), shape((8, width), full)], [], 7_000_000_000,
        (tokens, dfirst, dqkv, dgate, rate_back, rest, whole, fetched, vectors, table, chosen),
    )


def pack_kernel(block, table_ref, normed_ref, dlog_ref, sums_ref, more_ref, dw_ref, db_ref, dgain_ref, dshift_ref, rate_ref, rest_ref,
                chosen_ref, out_ref, held):
    width = sums_ref.shape[1]
    eta = dot_tn(dlog_ref[...], normed_ref[...])
    inner = dw_ref[:, :width] + dw_ref[:, width:]
    rows = jnp.concatenate(
        [inner, eta[ETA : ETA + 16], sums_ref[...] + more_ref[...], jnp.zeros((PAIR - VECTORS - 8, width), full)], axis=0
    )
    lane = lax.broadcasted_iota(jnp.int32, (HEAD, PAIR), 1)
    chosen = chosen_ref[...].astype(full)
    bias = jnp.sum(rate_ref[:, 0, :] * rest_ref[...], axis=0, keepdims=True)
    held[...] = rows.T
    bias = jnp.sum(chosen * bias, axis=1, keepdims=True)
    square = jnp.broadcast_to(bias, (PAIR, PAIR)).T[:1]
    bias_row = pltpu.roll(square, BIAS - ETA, axis=1)
    bias_row = jnp.where((lane[:1] >= BIAS) & (lane[:1] < BIAS + 12), bias_row, 0.0)
    for head in range(12):
        here = pl.ds(HEAD * head, HEAD)
        mask = chosen[ETA + head : ETA + head + 1]
        total = held[here, :] + bias_row
        for place, (ref, share) in enumerate(((db_ref, 1.0 / MINI), (dgain_ref, 1.0), (dshift_ref, 1.0))):
            column = jnp.sum(ref[...] * mask, axis=1, keepdims=True) * share
            total = total + jnp.where(lane == VECTORS + place, column, 0.0)
        held[here, :] = total
    store_blocks(table_ref, out_ref, held, block)


def pack(table, normed, dlog, sums, more, state, rate_back, rest, devices):
    rows, width = normed.shape
    _, chosen = lane_constants()
    spec = lambda array: constant_spec(*array.shape, buffers=1)
    arrays = (normed, dlog, sums, more, *state, rate_back, rest, chosen)
    return call(
        lambda *refs: pack_kernel(width // devices, *refs), "pack", (1,), 1,
        [spec(array) for array in arrays], constant_spec(width, PAIR, buffers=1), jax.ShapeDtypeStruct((width, PAIR), full),
        [pltpu.VMEM((width, PAIR), full)], 1_000_000_000, (table, *arrays),
    )


class Links:
    def __init__(self, dp, fsdp):
        self.axes = ("dp", "fsdp")
        self.count = dp * fsdp
        self.core = fsdp
        self.far = fsdp // 2
        bits = [1 << place for place in reversed(range(self.count.bit_length() - 1))]
        self.others = [bit for bit in bits if bit != self.core]
        near = [bit for bit in self.others if bit != self.far]
        self.orders = [near, near[1:] + near[:1]]
        self.phases = len(near)
        self.me = lax.axis_index("dp") * fsdp + lax.axis_index("fsdp")
        self.side = (self.me // self.core) % 2

    def swap(self, values, bits):
        pairs = [(place, place ^ bits[(place // self.core) % 2]) for place in range(self.count)]
        return lax.ppermute(values, self.axes, pairs)

    def gather(self, own, behind, at):
        orders = [[self.far] + order for order in self.orders]
        held = own
        for phase in range(len(orders[0])):
            if phase == at:
                held, behind = tie(held, behind)
            bits = [order[phase] for order in orders]
            got = self.swap(held, bits)
            ones = [(self.me // bit) % 2 for bit in bits]
            mine = jnp.where(self.side == 0, ones[0], ones[1]) == 0
            held = jnp.stack([jnp.where(mine, held, got), jnp.where(mine, got, held)])
        got = self.swap(held, [self.core] * 2)
        mine = self.side == 0
        pair = [jnp.where(mine, held, got), jnp.where(mine, got, held)]
        placed = []
        for array, order in zip(pair, orders):
            have = order[::-1]
            placed.append(array.transpose([have.index(bit) for bit in self.others] + [len(have), len(have) + 1]))
        above = [bit for bit in self.others if bit > self.core]
        return jnp.stack(placed, axis=len(above)).reshape(-1, own.shape[-1]), behind

    def tables(self):
        half = []
        for side in range(2):
            masks = self.orders[side] + [self.far]
            half.append(np.array([sum(bit for at, bit in enumerate(masks) if place >> (len(masks) - 1 - at) & 1)
                                  for place in range(self.count // 2)], np.int32))
        keep = jnp.where(self.side == 0, half[0], half[1])
        send = jnp.where(self.side == 0, half[1], half[0])
        table = jnp.concatenate([self.me ^ keep, self.me ^ self.core ^ send]).astype(jnp.int32)
        places = jnp.arange(self.count, dtype=jnp.int32)
        inverse = jnp.sum(jnp.where(table[None] == places[:, None], places[None], 0), axis=1).astype(jnp.int32)
        return table, inverse

    def scatter(self, arrays, wires):
        steps = [[self.core] * 2] + [list(pair) for pair in zip(*self.orders)] + [[self.far] * 2]
        for bits in steps:
            halves = [array.shape[0] // 2 for array in arrays]
            got = [self.swap(array[half:].astype(wire), bits) for array, half, wire in zip(arrays, halves, wires)]
            arrays = [array[:half].astype(full) + other.astype(full) for array, half, other in zip(arrays, halves, got)]
            changed = yield arrays
            arrays = arrays if changed is None else changed


def tie(*groups):
    flat, tree = jax.tree.flatten(groups)
    return jax.tree.unflatten(tree, lax.optimization_barrier(flat))


def in_order(table, array, rows):
    if rows % 8 == 0:
        return array
    return array.reshape((-1, rows) + array.shape[1:])[table].reshape(array.shape)


def body(dp, fsdp, tokens, lengths, cotangent, mixer_in, w_eta, eta_bias, w_out, inner_w, inner_b, ttt_gain, ttt_shift,
         norm_one, post_gain, post_shift, w_gate_up, w_down, norm_two):
    links = Links(dp, fsdp)
    devices = dp * fsdp
    micro, slots, width = tokens.shape
    rows = micro * slots
    heads = eta_bias.shape[0]
    head = width // heads
    hidden = w_gate_up.shape[1] // 2
    device_rows = width // devices
    table, inverse = links.tables()
    zeros = lambda columns: jnp.zeros((device_rows, columns), low)

    vectors = jnp.stack([inner_b, ttt_gain, ttt_shift, norm_one, post_gain, post_shift, norm_two])
    vectors = dot_tn(vectors, jnp.eye(7, PAIR, VECTORS, dtype=low)).astype(low)
    small = jnp.concatenate([inner_w, w_eta, zeros(PAIR - ETA - heads)], axis=1) + vectors
    parts = 3
    share = device_rows // parts
    piece = width // parts
    own_down = w_down.reshape(-1, share, parts, piece).transpose(2, 1, 0, 3).reshape(device_rows, hidden)
    own_rest = jnp.concatenate([mixer_in[:, 3 * width :], w_out, w_gate_up, own_down], axis=1)
    own = jnp.concatenate([mixer_in[:, : 3 * width], small], axis=1)
    whole, own_rest = links.gather(own, own_rest, 3)
    fetched = lax.all_gather(own_rest, ("dp", "fsdp"), axis=0, tiled=True)
    whole_down = fetched[:, 2 * width + 2 * hidden :].reshape(devices, parts, share, -1, piece).transpose(0, 3, 2, 1, 4)
    whole_down = whole_down.reshape(hidden, width)

    places = lax.broadcasted_iota(jnp.int32, (micro, slots), 1)
    live = places < lengths
    upstream = jnp.where(live[..., None], cotangent, jnp.zeros_like(cotangent)).reshape(rows, width)
    inputs = tokens.reshape(rows, width)
    bias_row = jnp.pad(eta_bias.astype(full), (ETA, PAIR - ETA - heads)).reshape(1, PAIR)
    projected, normed, rate_lanes, rest_lanes, start_w, start_b, gain_lanes, shift_lanes, vec_rows = project(
        lengths.reshape(micro), inputs, whole, bias_row
    )
    projected = projected.reshape(micro, slots, -1)
    inner, saved, _ = ttt_forward(projected, rate_lanes, [start_w, start_b], gain_lanes, shift_lanes)
    inner = inner.reshape(rows, width)
    gate, mixed, first, second = post(inner, normed, inputs, fetched, vec_rows)
    block_out, dsecond, grad_both, grad_down = ffn(
        table, inverse, second, first, upstream, fetched, whole_down, devices, dp
    )
    large_phases = links.scatter([in_order(table, grad_both, device_rows), grad_down], [low] * 2)
    large = next(large_phases)
    dsecond, large = tie(dsecond, large)
    large = large_phases.send(large)
    dfirst, dgate, dinner, sums, grad_middle = post_back(
        table, dsecond, first, upstream, inner, gate, mixed, normed, fetched, vec_rows, devices
    )
    middle_phases = links.scatter([in_order(table, grad_middle, device_rows)], [low])
    middle = next(middle_phases)
    dinner, middle = tie(dinner, middle)
    middle = middle_phases.send(middle)
    dinner = dinner.reshape(micro, slots, width)
    state = [jnp.zeros((HEAD, 1536), full)] + [jnp.zeros((HEAD, 384), full)] * 3
    dqkv, rate_back = None, []
    cuts = [32, 20, 12, 8, 0]
    for end, begin in zip(cuts[:-1], cuts[1:]):
        dqkv, rate_part, state = ttt_backward(
            projected, dinner, rate_lanes, saved, state, gain_lanes, begin, end, dqkv
        )
        rate_back.insert(0, rate_part)
        state, dqkv, large, middle = tie(state, dqkv, large, middle)
        large = next_or(large_phases, large)
        middle = next_or(middle_phases, middle)
    large, middle = drain(large_phases, large), drain(middle_phases, middle)
    dqkv = dqkv.reshape(rows, 3 * width)
    rate_back = jnp.concatenate(rate_back, axis=0)
    grad_mixer = in_order(table, weight_grads(table, normed, dqkv, devices), device_rows)
    last_phases = links.scatter([grad_mixer], [low])
    last = next(last_phases)
    dfirst, last = tie(dfirst, last)
    last = last_phases.send(last)
    grad_tokens, dlog, more = finish(inputs, dfirst, dqkv, dgate, rate_back, rest_lanes, whole, fetched, vec_rows)
    dlog, last = tie(dlog, last)
    last = last_phases.send(last)
    small_grad = pack(table, normed, dlog, sums, more, state, rate_back, rest_lanes, devices)
    small_grad, last = tie(small_grad, last)
    small_phases = links.scatter([in_order(table, small_grad, device_rows)], [full])
    last, (out_small,) = drain(last_phases, last_phases.send(last)), drain(small_phases, next(small_phases))
    out_inner_b, out_gain, out_shift, out_norm_one, out_post_gain, out_post_shift, out_norm_two = (
        out_small[:, VECTORS + place] for place in range(7)
    )
    out_out, out_gate_in = middle[0][:, :width], middle[0][:, width:]
    return (
        block_out.reshape(tokens.shape),
        grad_tokens.reshape(tokens.shape),
        jnp.concatenate([last[0], out_gate_in], axis=1),
        out_small[:, ETA : ETA + heads],
        out_small[0, BIAS : BIAS + heads],
        out_out,
        out_small[:, :head],
        out_inner_b,
        out_gain,
        out_shift,
        out_norm_one,
        out_post_gain,
        out_post_shift,
        large[0].reshape(device_rows, dp, 2, -1).transpose(0, 2, 1, 3).reshape(device_rows, 2 * hidden),
        large[1],
        out_norm_two,
    )


def next_or(phases, arrays):
    try:
        return phases.send(arrays)
    except StopIteration:
        return arrays


def drain(phases, arrays):
    for later in phases:
        arrays = later
    return arrays


def solution(mesh):
    split = ("dp", "fsdp")
    row, vector, token = P(split, None), P(split), P(None, split, None)
    dp, fsdp = mesh.shape["dp"], mesh.shape["fsdp"]
    return jax.shard_map(
        lambda *arrays: body(dp, fsdp, *arrays),
        mesh=mesh,
        in_specs=(token, P(None, split), token, row, row, P(), row, row) + (vector,) * 6 + (row, row, vector),
        out_specs=(token, token, row, row, P(), row, row) + (vector,) * 6 + (row, row, vector),
        check_vma=False,
    )
```

time: 3220 us -> 406 us (0.13)
  matrix products: 1220 us -> 0.88 us
  local copies, waits for them, and re-layouts: 715 us -> 37.7 us
  other arithmetic: 552 us -> 18.9 us
  waiting for transfers between devices: 432 us -> 70.6 us
  Pallas kernels: 0 us -> 231 us
  blocking collectives: 215 us -> 0 us
  loops' own time: 38.6 us -> 0 us
    dot_general x1374 -> x1, matrix products: 1220 us -> 0.88 us  [dot_tn(): lax.dot_general(former, latter, (((0,), (0,)), ((), ())), preferred_eleme...]
    reduce_scatter x4 -> x0, waiting for transfers between devices: 429 us -> none  [the longest x1 161 us: reduce_all(): lax.psum_scatter(ffn_terms[0], ('dp', 'fsdp'), scatter_dimension=0, tiled...]
    squeeze x320 -> x1, local copies, waits for them, and re-layouts: 281 us -> 0.58 us  [body(): out_small[0, BIAS:BIAS + heads]]
    pallas_call x0 -> x12, Pallas kernels: none -> 231 us  [the longest x7 114 us: call(): pl.pallas_call(kernel, grid_spec=pltpu.PrefetchScalarGridSpec(num_scalar_...]
    reduce_sum x775 -> x1, other arithmetic: 213 us -> 0.63 us  [tables(): jnp.sum(jnp.where(table[None] == places[:, None], places[None], 0), axis=1)]
    dynamic_update_slice x128 -> x0, other arithmetic: 160 us -> none  [inner_layer(): lax.scan(stepper, start, (split_heads(queries), split_heads(key_rows), sp...]
    all_gather x2 -> x0, blocking collectives: 139 us -> none  [the longest x1 71.9 us: fetch_mixer(): lax.all_gather(inner_w, ('dp', 'fsdp'), axis=0, tiled=True)]
    dynamic_update_slice x192 -> x0, local copies, waits for them, and re-layouts: 108 us -> none  [inner_layer(): lax.scan(stepper, start, (split_heads(queries), split_heads(key_rows), sp...]
where the time goes in v1:
time: 406 us; the launch traced here: 405 us
  Pallas kernels  231 us (57%)
  waiting for transfers between devices  70.6 us (17%)
  local copies, waits for them, and re-layouts  37.7 us (9%)
  starting transfers between devices  31.7 us (8%)
  other arithmetic  18.9 us (5%)
  between operations  14.8 us (4%)
    pallas_call x7, Pallas kernels, call(): pl.pallas_call(kernel, grid_spec=pltpu.PrefetchScalarGridSpec(num_scalar_...  114 us
    ppermute x30, waiting for transfers between devices, swap(): return lax.ppermute(values, self.axes, pairs)  70.6 us
    pallas_call x4, Pallas kernels, ttt_backward(): pl.pallas_call(lambda *refs: ttt_backward_kernel(steps, *refs), grid=(blo...  69.5 us
    pallas_call x1, Pallas kernels, ttt_forward(): pl.pallas_call(lambda *refs: ttt_forward_kernel(steps, *refs), grid=((end...  46.8 us
    ppermute x30, starting transfers between devices, swap(): return lax.ppermute(values, self.axes, pairs)  31.7 us
    unnamed x81, local copies, waits for them, and re-layouts  14.3 us
    add x25, other arithmetic, scatter(): array[:half].astype(full) + other.astype(full)  10.2 us
    slice x25, local copies, waits for them, and re-layouts, scatter(): array[half:].astype(wire)  9.85 us
  transfers between devices with their start and end apart: 31, of which 14 were waited for; matrix products, arithmetic and copies ran while one was open for 6% of the time, Pallas kernels for 36%

profile of v1, /device:TPU:0, one launch (start us, length us, event | category | flops | bytes accessed | tf_op | source)
XLA Modules:
  0.0 405.2 jit_solution(1725297396176763550)
XLA Ops:
  10.7 4.1 %collective-permute-start = (bf16[24,2432]{1,0:T(8,128)(2,1)S(1)}, bf16[24,2432]{1,0:T(8,128)(2,1)S(1)}, u32[]{:S(2)}, u32[]{:S(2)}) collective-permute-start(bf16[24,2432]{1,0:T(8,128)(2,1)S(1)} %pad_maximum_fusion.7), channel_id=1, source_target_pairs={{0,4},{1,5},{2,6},{3,7},{4,0},{5,1},{6,2},{7,3},{8,12},{9,13},{10,... | collective-permute-start | bytes 350216 | tf_op jit(solution)/shard_map/ppermute | solution.py:727
  14.8 5.7 %collective-permute-done = bf16[24,2432]{1,0:T(8,128)(2,1)S(1)} collective-permute-done((bf16[24,2432]{1,0:T(8,128)(2,1)S(1)}, bf16[24,2432]{1,0:T(8,128)(2,1)S(1)}, u32[]{:S(2)}, u32[]{:S(2)}) %collective-permute-start) | collective-permute-done | bytes 116768 | tf_op jit(solution)/shard_map/ppermute | solution.py:727
  28.4 7.1 %collective-permute-done.2 = bf16[2,2,24,2432]{3,2,1,0:T(8,128)(2,1)S(1)} collective-permute-done((bf16[2,2,24,2432]{3,2,1,0:T(8,128)(2,1)S(1)}, bf16[2,2,24,2432]{3,2,1,0:T(8,128)(2,1)S(1)}, u32[]{:S(2)}, u32[]{:S(2)}) %collective-permute-start.2) | collective-permute-done | bytes 466976 | tf_op jit(solution)/shard_map/ppermute | solution.py:727
  37.4 13.8 %collective-permute-done.3 = bf16[2,2,2,24,2432]{4,3,2,1,0:T(8,128)(2,1)} collective-permute-done((bf16[2,2,2,24,2432]{4,3,2,1,0:T(8,128)(2,1)S(1)}, bf16[2,2,2,24,2432]{4,3,2,1,0:T(8,128)(2,1)}, u32[]{:S(2)}, u32[]{:S(2)}) %collective-permute-start.3) | collective-permute-done | bytes 933920 | tf_op jit(solution)/shard_map/ppermute | solution.py:727
  63.0 12.3 %project.1 = (f32[1024,2432]{1,0:T(8,128)}, bf16[1024,768]{1,0:T(8,128)(2,1)}, f32[32,1,384]{2,1,0:T(1,128)}, f32[32,384]{1,0:T(8,128)}, f32[64,1536]{1,0:T(8,12...) custom-call(s32[2]{0:T(128)} %bitcast.91, bf16[1024,768]{1,0:T(8,128)(2,1)} %bitcast.81, ...), custom_call_target="tpu_custom_call" | custom-call | flops 5000000000 | bytes 10000000 | tf_op jit(solution)/shard_map/project/pallas_call | solution.py:362
  79.8 46.8 %ttt_forward.1 = (f32[2,512,768]{2,1,0:T(8,128)S(1)}, bf16[32,64,1536]{2,1,0:T(8,128)(2,1)}, f32[32,64,384]{2,1,0:T(8,128)S(1)}, f32[32,64,384]{2,1,0:T(8,128)S(...) custom-call(f32[2,512,2432]{2,1,0:T(8,128)} %bitcast.64, ...), custom_call_target="tpu_custom_call" | custom-call | flops 44800000000 | bytes 48000000 | tf_op jit(solution)/shard_map/ttt_forward/pallas_call | solution.py:275
  134.7 9.3 %post.1 = (f32[1024,768]{1,0:T(8,128)}, bf16[1024,768]{1,0:T(8,128)(2,1)}, f32[1024,768]{1,0:T(8,128)}, bf16[1024,768]{1,0:T(8,128)(2,1)}) custom-call(f32[1024,768]{1,0:T(8,128)} %bitcast.57, bf16[1024,768]{1,0:T(8,128)(2,1)} %get-tuple-element.126.normed_ref.refs_7_.refs_1_, bf16[1024,768]{1,0:T(8,128)(2,1)} %bitcast.82, ...), custom_call_target="tpu_custom_call" | custom-call | flops 4000000000 | bytes 8000000 | tf_op jit(solution)/shard_map/post/pallas_call | solution.py:362
  144.0 49.5 %ffn.1 = (bf16[1024,768]{1,0:T(8,128)(2,1)}, f32[1024,768]{1,0:T(8,128)}, bf16[768,4096]{1,0:T(8,128)(2,1)}, bf16[2048,768]{1,0:T(8,128)(2,1)}) custom-call(s32[32]{0:T(128)} %copy-done.31, s32[32]{0:T(128)} %select_reduce_fusion.refs_1_, bf16[1024,768]{1,0:T(8,128)(2,1)} %get-tuple-element.129.refs_2_, f32[1024,768]{1,0:T(8,128)} %get-tuple-element.130.refs_3_.refs_2_, ...), custom_call_target="tpu_custom_call" | custom-call | flops 28999999488 | bytes 58000000 | tf_op jit(solution)/shard_map/ffn/pallas_call | solution.py:362
  199.0 5.8 %collective-permute-done.6 = bf16[1024,768]{1,0:T(8,128)(2,1)S(1)} collective-permute-done((bf16[1024,768]{1,0:T(8,128)(2,1)S(1)}, bf16[1024,768]{1,0:T(8,128)(2,1)S(1)}, u32[]{:S(2)}, u32[]{:S(2)}) %collective-permute-start.6) | collective-permute-done | bytes 1572896 | tf_op jit(solution)/shard_map/ppermute | solution.py:727
  205.1 3.8 convert_add_fusion
  209.0 16.5 %post_back.1 = (f32[1024,768]{1,0:T(8,128)}, bf16[1024,768]{1,0:T(8,128)(2,1)}, f32[1024,768]{1,0:T(8,128)}, f32[8,768]{1,0:T(8,128)}, bf16[768,1536]{1,0:T(8,128)(2,1)}) custom-call(s32[32]{0:T(128)} %copy-done.31, f32[1024,768]{1,0:T(8,128)} %get-tuple-element.135.refs_1_, f32[1024,768]{1,0:T(8,128)} %get-tuple-element.130.refs_3_.refs_2_, ...), custom_call_target="tpu_custom_call" | custom-call | flops 5000000000 | bytes 10000000 | tf_op jit(solution)/shard_map/post_back/pallas_call | solution.py:362
  231.6 7.8 %collective-permute-done.9 = bf16[512,768]{1,0:T(8,128)(2,1)S(1)} collective-permute-done((bf16[512,768]{1,0:T(8,128)(2,1)S(1)}, bf16[512,768]{1,0:T(8,128)(2,1)S(1)}, u32[]{:S(2)}, u32[]{:S(2)}) %collective-permute-start.9) | collective-permute-done | bytes 786464 | tf_op jit(solution)/shard_map/ppermute | solution.py:727
  242.6 24.8 %ttt_backward.4 = (bf16[2,512,2304]{2,1,0:T(8,128)(2,1)}, f32[12,1,384]{2,1,0:T(1,128)S(1)}, f32[64,1536]{1,0:T(8,128)S(1)}, f32[64,384]{1,0:T(8,128)S(1)}, f32[...) custom-call(f32[2,512,2432]{2,1,0:T(8,128)} %bitcast.67, f32[2,512,2432]{2,1,0:T(8,128)} %bitcast.68, ...), custom_call_target="tpu_custom_call" | custom-call | flops 24000000000 | bytes 18000000 | tf_op jit(solution)/shard_map/ttt_backward/pallas_call | solution.py:306
  273.8 17.4 %ttt_backward.5 = (bf16[2,512,2304]{2,1,0:T(8,128)(2,1)}, f32[8,1,384]{2,1,0:T(1,128)S(1)}, f32[64,1536]{1,0:T(8,128)S(1)}, f32[64,384]{1,0:T(8,128)S(1)}, f32[64,384]{1,0:T(8,128)S(1)}, /*index=5*/f32[64,384]{1,0:T(8,128)S(1)}) custom-call(f32[2,512,2432]{2,1,0:T(8,128)} %bitcast.69, f32[2,512,2432]{2,1,0:T(8,128)} %bitcast.70, ...), custom_call_target="tpu_custom_call", output_to_operand_aliasing={{0}: (19, {})} | custom-call | flops 16000000000 | bytes 12000000 | tf_op jit(solution)/shard_map/ttt_backward/pallas_call | solution.py:306
  296.3 9.9 %ttt_backward.6 = (bf16[2,512,2304]{2,1,0:T(8,128)(2,1)}, f32[4,1,384]{2,1,0:T(1,128)S(1)}, f32[64,1536]{1,0:T(8,128)S(1)}, f32[64,384]{1,0:T(8,128)S(1)}, f32[64,384]{1,0:T(8,128)S(1)}, /*index=5*/f32[64,384]{1,0:T(8,128)S(1)}) custom-call(f32[2,512,2432]{2,1,0:T(8,128)} %bitcast.71, f32[2,512,2432]{2,1,0:T(8,128)} %bitcast.72, ...), custom_call_target="tpu_custom_call", output_to_operand_aliasing={{0}: (19, {})} | custom-call | flops 8000000000 | bytes 6000000 | tf_op jit(solution)/shard_map/ttt_backward/pallas_call | solution.py:306
  306.4 3.8 collective-permute-start.17
  313.3 17.3 %ttt_backward.7 = (bf16[2,512,2304]{2,1,0:T(8,128)(2,1)}, f32[8,1,384]{2,1,0:T(1,128)S(1)}, f32[64,1536]{1,0:T(8,128)S(1)}, f32[64,384]{1,0:T(8,128)S(1)}, f32[64,384]{1,0:T(8,128)S(1)}, /*index=5*/f32[64,384]{1,0:T(8,128)S(1)}) custom-call(f32[2,512,2432]{2,1,0:T(8,128)} %bitcast.73, f32[2,512,2432]{2,1,0:T(8,128)} %bitcast.74, ...), custom_call_target="tpu_custom_call", output_to_operand_aliasing={{0}: (19, {})} | custom-call | flops 16000000000 | bytes 12000000 | tf_op jit(solution)/shard_map/ttt_backward/pallas_call | solution.py:306
  334.1 11.2 %weight_grads.1 = bf16[768,2304]{1,0:T(8,128)(2,1)} custom-call(s32[32]{0:T(128)} %copy-done.31, bf16[1024,768]{1,0:T(8,128)(2,1)} %get-tuple-element.126.normed_ref.refs_7_.refs_1_, bf16[1024,2304]{1,0:T(8,128)(2,1)} %bitcast.75), custom_call_target="tpu_custom_call" | custom-call | flops 4000000000 | bytes 8000000 | tf_op jit(solution)/shard_map/weight_grads/pallas_call | solution.py:362
  347.2 3.7 collective-permute-done.20
  353.5 11.5 %finish.1 = (bf16[1024,768]{1,0:T(8,128)(2,1)}, bf16[1024,128]{1,0:T(8,128)(2,1)}, f32[8,768]{1,0:T(8,128)}) custom-call(bf16[1024,768]{1,0:T(8,128)(2,1)} %bitcast.83, f32[1024,768]{1,0:T(8,128)} %get-tuple-element.197.dfirst_ref, bf16[1024,2304]{1,0:T(8,128)(2,1)} %bitcast.76, bf16[1024,768]{1,0:T(8,128)(2,1)} %get-tuple-element.198.dgate_ref, ...), custom_call_target="tpu_custom_call" | custom-call | flops 7000000000 | bytes 14000000 | tf_op jit(solution)/shard_map/finish/pallas_call | solution.py:362
  365.4 4.0 pack.1
  369.4 4.2 %collective-permute-done.22 = bf16[96,2304]{1,0:T(8,128)(2,1)S(1)} collective-permute-done((bf16[96,2304]{1,0:T(8,128)(2,1)S(1)}, bf16[96,2304]{1,0:T(8,128)(2,1)S(1)}, u32[]{:S(2)}, u32[]{:S(2)}) %collective-permute-start.22) | collective-permute-done | bytes 442400 | tf_op jit(solution)/shard_map/ppermute | solution.py:727
  380.1 4.7 %collective-permute-done.23 = bf16[48,2304]{1,0:T(8,128)(2,1)S(1)} collective-permute-done((bf16[48,2304]{1,0:T(8,128)(2,1)S(1)}, bf16[48,2304]{1,0:T(8,128)(2,1)S(1)}, u32[]{:S(2)}, u32[]{:S(2)}) %collective-permute-start.23) | collective-permute-done | bytes 221216 | tf_op jit(solution)/shard_map/ppermute | solution.py:727
  385.2 6.2 %collective-permute-done.24 = bf16[24,2304]{1,0:T(8,128)(2,1)S(1)} collective-permute-done((bf16[24,2304]{1,0:T(8,128)(2,1)S(1)}, bf16[24,2304]{1,0:T(8,128)(2,1)S(1)}, u32[]{:S(2)}, u32[]{:S(2)}) %collective-permute-start.24) | collective-permute-done | bytes 110624 | tf_op jit(solution)/shard_map/ppermute | solution.py:727
  (227 shorter events, 89.1 us)
Async XLA Ops:
  7.2 123.7 %all-gather.2.cloned.1.call-start = ((), (), s32[]{:S(2)}) async-start(), calls=%async_computation | async-start | bytes 12165120 | tf_op jit(solution)/shard_map/all_gather | solution.py:807
  10.7 9.8 %collective-permute-start = (bf16[24,2432]{1,0:T(8,128)(2,1)S(1)}, bf16[24,2432]{1,0:T(8,128)(2,1)S(1)}, u32[]{:S(2)}, u32[]{:S(2)}) collective-permute-start(bf16[24,2432]{1,0:T(8,128)(2,1)S(1)} %pad_maximum_fusion.7), channel_id=1, source_target_pairs={{0,4},{1,5},{2,6},{3,7},{4,0},{5,1},{6,2},{7,3},{8,12},{9,13},{10,... | collective-permute-start | bytes 350216 | tf_op jit(solution)/shard_map/ppermute | solution.py:727
  20.6 6.1 %collective-permute-start.1 = (bf16[2,24,2432]{2,1,0:T(8,128)(2,1)S(1)}, bf16[2,24,2432]{2,1,0:T(8,128)(2,1)S(1)}, u32[]{:S(2)}, u32[]{:S(2)}) collective-permute-start(bf16[2,24,2432]{2,1,0:T(8,128)(2,1)S(1)} %pad_maximum_fusion.6), channel_id=1, source_target_pairs={{0,16},{1,17},{2,18},{3,19},{4,20},{5,21},{6,22},{7,23},{8,10},{9,... | collective-permute-start | bytes 700424 | tf_op jit(solution)/shard_map/ppermute | solution.py:727
  26.9 8.6 %collective-permute-start.2 = (bf16[2,2,24,2432]{3,2,1,0:T(8,128)(2,1)S(1)}, bf16[2,2,24,2432]{3,2,1,0:T(8,128)(2,1)S(1)}, u32[]{:S(2)}, u32[]{:S(2)}) collective-permute-start(bf16[2,2,24,2432]{3,2,1,0:T(8,128)(2,1)S(1)} %pad_maximum_fusion.3), channel_id=1, source_target_pairs={{0,2},{1,3},{2,0},{3,1},{4,6},{5,7},{6,4},{7,5},{8,9},{9,8},{10,11... | collective-permute-start | bytes 1400840 | tf_op jit(solution)/shard_map/ppermute | solution.py:727
  35.7 15.4 %collective-permute-start.3 = (bf16[2,2,2,24,2432]{4,3,2,1,0:T(8,128)(2,1)S(1)}, bf16[2,2,2,24,2432]{4,3,2,1,0:T(8,128)(2,1)}, u32[]{:S(2)}, u32[]{:S(2)}) collective-permute-start(bf16[2,2,2,24,2432]{4,3,2,1,0:T(8,128)(2,1)S(1)} %pad_maximum_fusion.2), channel_id=1, source_target_pairs={{0,1},{1,0},{2,3},{3,2},{4,5},{5,4},{6,7},{7,6},{8,24},{9,25},{10,... | collective-permute-start | bytes 2801672 | tf_op jit(solution)/shard_map/ppermute | solution.py:727
  195.8 9.3 %collective-permute-start.5 = (bf16[384,4096]{1,0:T(8,128)(2,1)S(1)}, bf16[384,4096]{1,0:T(8,128)(2,1)S(1)}, u32[]{:S(2)}, u32[]{:S(2)}) collective-permute-start(bf16[384,4096]{1,0:T(8,128)(2,1)S(1)} %slice.215), channel_id=1, source_target_pairs={{0,8},{1,9},{2,10},{3,11},{4,12},{5,13},{6,14},{7,15},{8,0},{9,1},... | collective-permute-start | bytes 9437192 | tf_op jit(solution)/shard_map/ppermute | solution.py:727
  226.8 12.8 %collective-permute-start.7 = (bf16[384,1536]{1,0:T(8,128)(2,1)S(1)}, bf16[384,1536]{1,0:T(8,128)(2,1)S(1)}, u32[]{:S(2)}, u32[]{:S(2)}) collective-permute-start(bf16[384,1536]{1,0:T(8,128)(2,1)S(1)} %slice.219), channel_id=1, source_target_pairs={{0,8},{1,9},{2,10},{3,11},{4,12},{5,13},{6,14},{7,15},{8,0},{9,1},... | collective-permute-start | bytes 3538952 | tf_op jit(solution)/shard_map/ppermute | solution.py:727
  227.3 12.1 %collective-permute-start.9 = (bf16[512,768]{1,0:T(8,128)(2,1)S(1)}, bf16[512,768]{1,0:T(8,128)(2,1)S(1)}, u32[]{:S(2)}, u32[]{:S(2)}) collective-permute-start(bf16[512,768]{1,0:T(8,128)(2,1)S(1)} %slice.366), channel_id=1, source_target_pairs={{0,16},{1,17},{2,18},{3,19},{4,20},{5,21},{6,22},{7,23},{8,10},{9,... | collective-permute-start | bytes 2359304 | tf_op jit(solution)/shard_map/ppermute | solution.py:727
  231.2 36.2 %collective-permute-start.8 = (bf16[192,4096]{1,0:T(8,128)(2,1)S(1)}, bf16[192,4096]{1,0:T(8,128)(2,1)S(1)}, u32[]{:S(2)}, u32[]{:S(2)}) collective-permute-start(bf16[192,4096]{1,0:T(8,128)(2,1)S(1)} %slice.363), channel_id=1, source_target_pairs={{0,16},{1,17},{2,18},{3,19},{4,20},{5,21},{6,22},{7,23},{8,10},{9,... | collective-permute-start | bytes 4718600 | tf_op jit(solution)/shard_map/ppermute | solution.py:727
  240.0 29.8 %collective-permute-start.10 = (bf16[192,1536]{1,0:T(8,128)(2,1)S(1)}, bf16[192,1536]{1,0:T(8,128)(2,1)}, u32[]{:S(2)}, u32[]{:S(2)}) collective-permute-start(bf16[192,1536]{1,0:T(8,128)(2,1)S(1)} %slice.367), channel_id=1, source_target_pairs={{0,16},{1,17},{2,18},{3,19},{4,20},{5,21},{6,22},{7,23},{8,10},{9,... | collective-permute-start | bytes 1769480 | tf_op jit(solution)/shard_map/ppermute | solution.py:727
  271.1 20.2 %collective-permute-start.11 = (bf16[96,4096]{1,0:T(8,128)(2,1)S(1)}, bf16[96,4096]{1,0:T(8,128)(2,1)S(1)}, u32[]{:S(2)}, u32[]{:S(2)}) collective-permute-start(bf16[96,4096]{1,0:T(8,128)(2,1)S(1)} %slice.365), channel_id=1, source_target_pairs={{0,2},{1,3},{2,0},{3,1},{4,6},{5,7},{6,4},{7,5},{8,9},{9,8},{10,11... | collective-permute-start | bytes 2359304 | tf_op jit(solution)/shard_map/ppermute | solution.py:727
  271.6 19.6 %collective-permute-start.12 = (bf16[256,768]{1,0:T(8,128)(2,1)S(1)}, bf16[256,768]{1,0:T(8,128)(2,1)S(1)}, u32[]{:S(2)}, u32[]{:S(2)}) collective-permute-start(bf16[256,768]{1,0:T(8,128)(2,1)S(1)} %slice.370), channel_id=1, source_target_pairs={{0,2},{1,3},{2,0},{3,1},{4,6},{5,7},{6,4},{7,5},{8,9},{9,8},{10,11... | collective-permute-start | bytes 1179656 | tf_op jit(solution)/shard_map/ppermute | solution.py:727
  273.3 17.8 %collective-permute-start.13 = (bf16[96,1536]{1,0:T(8,128)(2,1)S(1)}, bf16[96,1536]{1,0:T(8,128)(2,1)S(1)}, u32[]{:S(2)}, u32[]{:S(2)}) collective-permute-start(bf16[96,1536]{1,0:T(8,128)(2,1)S(1)} %slice.371), channel_id=1, source_target_pairs={{0,2},{1,3},{2,0},{3,1},{4,6},{5,7},{6,4},{7,5},{8,9},{9,8},{10,11... | collective-permute-start | bytes 884744 | tf_op jit(solution)/shard_map/ppermute | solution.py:727
  291.5 14.8 %collective-permute-start.14 = (bf16[48,4096]{1,0:T(8,128)(2,1)S(1)}, bf16[48,4096]{1,0:T(8,128)(2,1)S(1)}, u32[]{:S(2)}, u32[]{:S(2)}) collective-permute-start(bf16[48,4096]{1,0:T(8,128)(2,1)S(1)} %slice.369), channel_id=1, source_target_pairs={{0,1},{1,0},{2,3},{3,2},{4,5},{5,4},{6,7},{7,6},{8,24},{9,25},{10,... | collective-permute-start | bytes 1179656 | tf_op jit(solution)/shard_map/ppermute | solution.py:727
  294.1 12.2 %collective-permute-start.15 = (bf16[128,768]{1,0:T(8,128)(2,1)S(1)}, bf16[128,768]{1,0:T(8,128)(2,1)S(1)}, u32[]{:S(2)}, u32[]{:S(2)}) collective-permute-start(bf16[128,768]{1,0:T(8,128)(2,1)S(1)} %slice.374), channel_id=1, source_target_pairs={{0,1},{1,0},{2,3},{3,2},{4,5},{5,4},{6,7},{7,6},{8,24},{9,25},{10,... | collective-permute-start | bytes 589832 | tf_op jit(solution)/shard_map/ppermute | solution.py:727
  294.2 12.0 %collective-permute-start.16 = (bf16[48,1536]{1,0:T(8,128)(2,1)S(1)}, bf16[48,1536]{1,0:T(8,128)(2,1)S(1)}, u32[]{:S(2)}, u32[]{:S(2)}) collective-permute-start(bf16[48,1536]{1,0:T(8,128)(2,1)S(1)} %slice.375), channel_id=1, source_target_pairs={{0,1},{1,0},{2,3},{3,2},{4,5},{5,4},{6,7},{7,6},{8,24},{9,25},{10,... | collective-permute-start | bytes 442376 | tf_op jit(solution)/shard_map/ppermute | solution.py:727
  306.4 27.6 %collective-permute-start.17 = (bf16[24,4096]{1,0:T(8,128)(2,1)S(1)}, bf16[24,4096]{1,0:T(8,128)(2,1)S(1)}, u32[]{:S(2)}, u32[]{:S(2)}) collective-permute-start(bf16[24,4096]{1,0:T(8,128)(2,1)S(1)} %slice.373), channel_id=1, source_target_pairs={{0,4},{1,5},{2,6},{3,7},{4,0},{5,1},{6,2},{7,3},{8,12},{9,13},{10,... | collective-permute-start | bytes 589832 | tf_op jit(solution)/shard_map/ppermute | solution.py:727
  310.2 23.1 %collective-permute-start.18 = (bf16[64,768]{1,0:T(8,128)(2,1)S(1)}, bf16[64,768]{1,0:T(8,128)(2,1)S(1)}, u32[]{:S(2)}, u32[]{:S(2)}) collective-permute-start(bf16[64,768]{1,0:T(8,128)(2,1)S(1)} %slice.377), channel_id=1, source_target_pairs={{0,4},{1,5},{2,6},{3,7},{4,0},{5,1},{6,2},{7,3},{8,12},{9,13},{10,... | collective-permute-start | bytes 294920 | tf_op jit(solution)/shard_map/ppermute | solution.py:727
  310.3 23.0 %collective-permute-start.19 = (bf16[24,1536]{1,0:T(8,128)(2,1)S(1)}, bf16[24,1536]{1,0:T(8,128)(2,1)S(1)}, u32[]{:S(2)}, u32[]{:S(2)}) collective-permute-start(bf16[24,1536]{1,0:T(8,128)(2,1)S(1)} %slice.378), channel_id=1, source_target_pairs={{0,4},{1,5},{2,6},{3,7},{4,0},{5,1},{6,2},{7,3},{8,12},{9,13},{10,... | collective-permute-start | bytes 221192 | tf_op jit(solution)/shard_map/ppermute | solution.py:727
  351.3 13.7 %collective-permute-start.21 = (bf16[192,2304]{1,0:T(8,128)(2,1)S(1)}, bf16[192,2304]{1,0:T(8,128)(2,1)S(1)}, u32[]{:S(2)}, u32[]{:S(2)}) collective-permute-start(bf16[192,2304]{1,0:T(8,128)(2,1)S(1)} %slice.364), channel_id=1, source_target_pairs={{0,16},{1,17},{2,18},{3,19},{4,20},{5,21},{6,22},{7,23},{8,10},{9,... | collective-permute-start | bytes 2654216 | tf_op jit(solution)/shard_map/ppermute | solution.py:727
  365.2 8.4 %collective-permute-start.22 = (bf16[96,2304]{1,0:T(8,128)(2,1)S(1)}, bf16[96,2304]{1,0:T(8,128)(2,1)S(1)}, u32[]{:S(2)}, u32[]{:S(2)}) collective-permute-start(bf16[96,2304]{1,0:T(8,128)(2,1)S(1)} %slice.368), channel_id=1, source_target_pairs={{0,2},{1,3},{2,0},{3,1},{4,6},{5,7},{6,4},{7,5},{8,9},{9,8},{10,11... | collective-permute-start | bytes 1327112 | tf_op jit(solution)/shard_map/ppermute | solution.py:727
  378.3 6.5 %collective-permute-start.23 = (bf16[48,2304]{1,0:T(8,128)(2,1)S(1)}, bf16[48,2304]{1,0:T(8,128)(2,1)S(1)}, u32[]{:S(2)}, u32[]{:S(2)}) collective-permute-start(bf16[48,2304]{1,0:T(8,128)(2,1)S(1)} %slice.372), channel_id=1, source_target_pairs={{0,1},{1,0},{2,3},{3,2},{4,5},{5,4},{6,7},{7,6},{8,24},{9,25},{10,... | collective-permute-start | bytes 663560 | tf_op jit(solution)/shard_map/ppermute | solution.py:727
  384.9 6.5 %collective-permute-start.24 = (bf16[24,2304]{1,0:T(8,128)(2,1)S(1)}, bf16[24,2304]{1,0:T(8,128)(2,1)S(1)}, u32[]{:S(2)}, u32[]{:S(2)}) collective-permute-start(bf16[24,2304]{1,0:T(8,128)(2,1)S(1)} %slice.376), channel_id=1, source_target_pairs={{0,4},{1,5},{2,6},{3,7},{4,0},{5,1},{6,2},{7,3},{8,12},{9,13},{10,... | collective-permute-start | bytes 331784 | tf_op jit(solution)/shard_map/ppermute | solution.py:727
  385.0 6.4 %collective-permute-start.28 = (f32[48,128]{1,0:T(8,128)S(1)}, f32[48,128]{1,0:T(8,128)S(1)}, u32[]{:S(2)}, u32[]{:S(2)}) collective-permute-start(f32[48,128]{1,0:T(8,128)S(1)} %slice.301), channel_id=1, source_target_pairs={{0,1},{1,0},{2,3},{3,2},{4,5},{5,4},{6,7},{7,6},{8,24},{9,25},{10,... | collective-permute-start | bytes 73736 | tf_op jit(solution)/shard_map/ppermute | solution.py:727
  (47 other events, 218.5 us)
Sparse Core Ops, SparseCore 0:
  35.9 94.4 all-gather.1
